TPU v7x, 128 devices: a whole 4x4x4 slice. The times are simulated.
128 devices in a mesh: grp: 8 (over x, core), dom: 16 (over z, y).
Axes of the slice: x: 4, y: 4, z: 4, core: 2. Of those that a mesh axis runs over, the one named last changes fastest.
Arguments:
- pattern: int32 [256, 16], replicated, may hold values from 0 to 255, as said below
- density: bfloat16 [256, 16, 128, 128], P(('grp', 'dom')), may hold values from -1 to 1
- hamiltonian: bfloat16 [256, 16, 128, 128], P(('grp', 'dom')), may hold values from -1 to 1
Outputs:
- purified: float32 [256, 16, 128, 128], P(('grp', 'dom'))
- gradient: float32 [256, 16, 128, 128], P(('grp', 'dom'))
Inputs may be any that keep to these rules, and one draw needn't show every extreme that they name: `pattern`: slot 0 of block row i is i itself. Slot 1 is a block row of the previous domain group (cyclically) and slot 2 one of the next, each held by the device of the same dom index; the other slots are distinct block rows of the row's own domain group other than i. Block rows are numbered group by group, device by device, 2 to a device.
All inputs are finite; a program needn't handle non-finite values.
Results may differ from a plain program's by a relative error of at most 0.0028.
Values may be sent and summed in bfloat16 or wider, within the bound.
A program may use at most 192 MiB of HBM per device.

v0:
```python
import functools

import jax
import jax.numpy as jnp
from jax import lax
from jax.experimental import pallas as pl
from jax.experimental.pallas import tpu as pltpu
from jax.sharding import PartitionSpec as P

MESH = pl.DeviceIdType.MESH
BLK = 128
NNZ = 16
KEPT = 14
SPAN = 32
GROUPS = 8
EXTRA = SPAN * KEPT
TOTAL = EXTRA + 4 + 6 + 6
CUT = 6
ZH = CUT // 2
CHUNK = 2
STEP = 8
ENTRIES = NNZ * NNZ
YH = CUT + (KEPT - CUT) // 2
PARTS = ((CUT + 2, NNZ, CUT), (0, 1, 0), (3, CUT + 2, 1))

EVENTS = {
    "Zp": ((0, CUT), 0, 0, "zp"),
    "Zm": ((0, CUT), 0, 0, "zm"),
    "ZpF": ((0, ZH), -1, 0, "zp"),
    "ZmF": ((ZH, CUT), 1, 0, "zm"),
    "ZY0": ((0, CUT), 0, 0, "y"),
    "ZYm": ((0, CUT), -1, 0, "y"),
    "ZYp": ((0, CUT), 1, 0, "y"),
    "ZYa": ((0, ZH), 2, 0, "y"),
    "ZYb": ((ZH, CUT), 2, 0, "y"),
    "Y": ((CUT, KEPT), 0, 0, "y"),
    "Yp": ((CUT, KEPT), 0, 0, "zp"),
    "Ym": ((CUT, KEPT), 0, 0, "zm"),
    "YpF": ((CUT, YH), -1, 0, "zp"),
    "YmF": ((YH, KEPT), 1, 0, "zm"),
    "Xp": ((CUT, KEPT), 0, 1, "zp"),
    "Xm": ((CUT, KEPT), 0, 1, "zm"),
    "XpF": ((CUT, YH), -1, 1, "zp"),
    "XmF": ((YH, KEPT), 1, 1, "zm"),
}
NAMES = tuple(EVENTS)
N_EV = len(NAMES)
ORDER = (
    "R Zp O", "R Zm O", "S ZpF O", "S ZmF O", "R Y O", "S Xp O", "S Xm O", "QY",
    "S Y Q", "S Yp Q", "S Ym Q", "S ZY0 O", "S ZYm O", "S ZYp O", "R Yp O", "R Ym O",
    "S YpF O", "S YmF O", "QZ", "S Zp Q", "S Zm Q", "R Y Q", "S Xp Q", "S Xm Q",
    "R ZpF O", "R ZmF O", "S ZYa O", "S ZYb O", "S ZY0 Q", "R Xp O", "R Xm O", "S XpF O",
    "S XmF O", "R YpF O", "R YmF O", "R ZY0 O", "R Yp Q", "R Ym Q", "S YpF Q", "S YmF Q",
    "R Zp Q", "R Zm Q", "S ZpF Q", "S ZmF Q", "S ZYm Q", "S ZYp Q", "R ZYm O", "R Xp Q",
    "R Xm Q", "S XpF Q", "S XmF Q", "R ZpF Q", "R ZmF Q", "S ZYa Q", "S ZYb Q", "R ZYp O",
    "R XpF O", "R XmF O", "R YpF Q", "R YmF Q", "R ZYa O", "R ZYb O", "R ZY0 Q", "R ZYm Q",
    "R ZYp Q", "R XpF Q", "R XmF Q", "R ZYa Q", "R ZYb Q",
)


def gather_kernel(
    p_ref, h_ref, all_ref,
    ss, rs, ds, dr, loc, ins, inr, qs, qr, es, er, xs, xr,
):
    args = (p_ref, h_ref)
    g, d = lax.axis_index("grp"), lax.axis_index("dom")
    x, c = g // 2, g % 2
    z, y = d // 4, d % 4
    host = y // 2
    yn, yq = y + 1 - 2 * (y % 2), 3 - y
    dq = z * 4 + yq
    sib_g = g + 1 - 2 * c
    sibling = (sib_g, d)
    ways = {
        "zp": (g, (z + 1) % 4 * 4 + y),
        "zm": (g, (z + 3) % 4 * 4 + y),
        "y": (g, z * 4 + yn),
    }
    is_own = (c + host + 1) % 2
    work_g = is_own * g + (1 - is_own) * sib_g
    work_d = is_own * d + (1 - is_own) * dq
    up, down = (g + 1) % GROUPS, (g + GROUPS - 1) % GROUPS
    up_t = (is_own * (up + 1 - 2 * (up % 2)) + (1 - is_own) * up, is_own * dq + (1 - is_own) * d)
    down_t = (is_own * (down + 1 - 2 * (down % 2)) + (1 - is_own) * down, is_own * dq + (1 - is_own) * d)
    partner_idle = (2 * x + host, dq)

    barrier = pltpu.get_barrier_semaphore()
    for who in (
        *ways.values(), sibling, partner_idle,
        ((work_g + GROUPS - 1) % GROUPS, work_d), ((work_g + 1) % GROUPS, work_d),
    ):
        pl.semaphore_signal(barrier, inc=1, device_id=who, device_id_type=MESH)
    pl.semaphore_wait(barrier, 8 - 2 * is_own)

    def at(dom, row, lo, n):
        return all_ref.at[pl.ds((dom * 2 + row) * KEPT + lo, n)]

    def at1(dom, row, lo, n, a):
        return all_ref.at[pl.ds((dom * 2 + row) * KEPT + lo, n), a]

    def remote(src, dst, s, r, who):
        return pltpu.make_async_remote_copy(
            src_ref=src, dst_ref=dst, send_sem=s, recv_sem=r, device_id=who, device_id_type=MESH
        )

    def init_copies(row, to):
        out = []
        for k, (s0, s1, b) in enumerate(PARTS):
            for a in range(2):
                src = args[a].at[row, pl.ds(s0, s1 - s0)]
                dst = at1(d, row, b, s1 - s0, a)
                if to == "own":
                    out.append(pltpu.make_async_copy(src, dst, loc.at[row, k, a]))
                elif to == "sibling":
                    out.append(remote(src, dst, ins.at[row, k, a], inr.at[row, k, a], sibling))
                else:
                    out.append(remote(src, dst, qs.at[row, k, a], qr.at[k, a], (2 * x + row, dq)))
        return out

    def extra_copies(to):
        out = []
        for row in range(2):
            for a in range(2):
                src = args[a].at[row, pl.ds(1, 2)]
                dst = all_ref.at[pl.ds(EXTRA + 2 * row, 2), a]
                if to == "own":
                    out.append(pltpu.make_async_copy(src, dst, es.at[row, a]))
                else:
                    out.append(remote(src, dst, es.at[row, a], er.at[row, a], (sib_g, dq)))
        return out

    def side_copies():
        out = []
        for k, who in enumerate((up_t, down_t)):
            for row in range(2):
                for a in range(2):
                    src = args[a].at[row, pl.ds(0, 3)]
                    dst = all_ref.at[pl.ds(EXTRA + 4 + 6 * k + 3 * row, 3), a]
                    out.append(remote(src, dst, xs.at[k, row, a], xr.at[k, row, a], who))
        return out

    own = c == host
    for core in range(2):

        @pl.when(jnp.logical_and(own, c == core))
        def _():
            mine = init_copies(core, "own")
            theirs = init_copies(1 - core, "sibling")
            for m, t in zip(mine, theirs):
                m.start()
                t.start()
            for copy in init_copies(core, "sibling") + init_copies(1 - core, "own"):
                copy.start()
            for copy in mine:
                copy.wait()

        @pl.when(jnp.logical_and(jnp.logical_not(own), c == core))
        def _():
            for m, t in zip(init_copies(0, "partner"), init_copies(1, "partner")):
                m.start()
                t.start()
            for copy in init_copies(core, "sibling"):
                copy.wait_recv()

    def dom_of(zz, col, kind):
        yy = y if col == 0 else yn
        return (z + zz + 4) % 4 * 4 + (yy if kind == "O" else 3 - yy)

    def event(name, kind, side):
        (lo, hi), zz, col, way = EVENTS[name]
        k = NAMES.index(name) + (N_EV if kind == "Q" else 0)
        if side == "R":
            if way == "zp":
                zz -= 1
            elif way == "zm":
                zz += 1
            else:
                col = 1
        dom = dom_of(zz, col, kind)
        ref = at(dom, c, lo, hi - lo)
        return remote(ref, ref, ss.at[k], rs.at[k], ways[way]), (dom, lo, hi - lo, k)

    passed = []

    def to_sibling(dom, lo, n, k):
        ref = at(dom, c, lo, n)
        remote(ref, ref, ds.at[k], dr.at[k], sibling).start()
        passed.append((dom, lo, n, k))

    sent = []

    def send(name, kind):
        copy, _ = event(name, kind, "S")
        copy.start()
        sent.append(copy)

    def receive(name, kind):
        copy, what = event(name, kind, "R")
        copy.wait_recv()
        to_sibling(*what)

    def receive_partner(parts, lo, n, k):
        for part in parts:
            s0, s1, b = PARTS[part]
            for a in range(2):
                ref = at1(dq, c, b, s1 - s0, a)
                remote(ref, ref, qs.at[0, part, a], qr.at[part, a], sibling).wait_recv()
        to_sibling(dq, lo, n, k)

    for name in ("Y", "Zp", "Zm", "Yp", "Ym"):
        send(name, "O")

    sides = side_copies()
    for copy in sides:
        copy.start()

    @pl.when(own)
    def _():
        for copy in extra_copies("own"):
            copy.start()

    @pl.when(jnp.logical_not(own))
    def _():
        for copy in extra_copies("partner"):
            copy.start()

    for step in ORDER:
        if step == "QY":
            receive_partner((0,), CUT, KEPT - CUT, 2 * N_EV)
        elif step == "QZ":
            receive_partner((1, 2), 0, CUT, 2 * N_EV + 1)
        else:
            what, name, kind = step.split()
            (send if what == "S" else receive)(name, kind)

    for core in range(2):

        @pl.when(jnp.logical_and(own, c == core))
        def _():
            for copy in init_copies(1 - core, "own") + extra_copies("own"):
                copy.wait()
            for copy in init_copies(0, "sibling") + init_copies(1, "sibling"):
                copy.wait_send()

        @pl.when(jnp.logical_and(jnp.logical_not(own), c == core))
        def _():
            for copy in init_copies(1 - core, "sibling"):
                copy.wait_recv()
            for copy in init_copies(0, "partner") + init_copies(1, "partner"):
                copy.wait_send()
            for copy in extra_copies("partner"):
                copy.wait()

    for copy in sides:
        copy.wait()
    for copy in sent:
        copy.wait_send()
    for dom, lo, n, k in passed:
        mine, theirs = at(dom, c, lo, n), at(dom, 1 - c, lo, n)
        remote(mine, mine, ds.at[k], dr.at[k], sibling).wait_send()
        remote(theirs, theirs, ds.at[k], dr.at[k], sibling).wait_recv()


def gather(density, hamiltonian):
    dma = pltpu.SemaphoreType.DMA
    return pl.pallas_call(
        gather_kernel,
        name="gather",
        out_shape=jax.ShapeDtypeStruct((TOTAL, 2, BLK, BLK), jnp.bfloat16),
        in_specs=[pl.BlockSpec(memory_space=pl.ANY)] * 2,
        out_specs=pl.BlockSpec(memory_space=pl.ANY),
        scratch_shapes=[
            dma((2 * N_EV,)), dma((2 * N_EV,)), dma((2 * N_EV + 2,)), dma((2 * N_EV + 2,)),
            dma((2, 3, 2)), dma((2, 3, 2)), dma((2, 3, 2)), dma((2, 3, 2)), dma((3, 2)),
            dma((2, 2)), dma((2, 2)), dma((2, 2, 2)), dma((2, 2, 2)),
        ],
        compiler_params=pltpu.CompilerParams(collective_id=0, has_side_effects=True),
    )(density, hamiltonian)


def row_kernel(
    steps, chunk_s, slots, places, mine, all_ref, x_ref, g_ref, send_ref,
    left, right, low, high, mid, sem_a, sem_b,
):
    def fetch_left(lo, n, at):
        return pltpu.make_async_copy(
            all_ref.at[pl.ds(at, n)], left.at[pl.ds(lo, n)], sem_a.at[lo // KEPT]
        )

    def fetch(e):
        return pltpu.make_async_copy(all_ref.at[places[e]], right.at[e], sem_b.at[e])

    def fetch_step(q, what):
        for k in range(STEP * CHUNK):
            what(fetch(q * (STEP * CHUNK) + k))

    a_copies = (fetch_left(0, KEPT, mine[0]), fetch_left(KEPT, 2, mine[1]))
    for copy in a_copies:
        copy.start()

    @pl.loop(0, steps[0])
    def _(q):
        fetch_step(q, lambda copy: copy.start())

    left[NNZ] = jnp.zeros((2, BLK, BLK), jnp.bfloat16)
    mid[NNZ] = jnp.zeros((2, BLK, BLK), jnp.bfloat16)
    for s in range(NNZ):
        low[s] = jnp.zeros((BLK, 2 * BLK), jnp.float32)
        high[s] = jnp.zeros((BLK, 2 * BLK), jnp.float32)
    for copy in a_copies:
        copy.wait()

    def step(q, a_ref, total):
        sums = []
        for k in range(STEP):
            first = (q * STEP + k) * CHUNK
            e = [first + p for p in range(CHUNK)]
            t = [slots[p] for p in e]
            a = jnp.concatenate([a_ref[p, 0] for p in t], axis=1)
            b = jnp.concatenate([a_ref[p, 1] for p in t], axis=1)
            den = jnp.concatenate([right[p, 0] for p in e], axis=0)
            ham = jnp.concatenate([right[p, 1] for p in e], axis=0)
            both = jnp.dot(a, jnp.concatenate([den, ham], axis=1), preferred_element_type=jnp.float32)
            more = jnp.dot(b, den, preferred_element_type=jnp.float32)
            sums.append((both, more))
        for k in range(STEP):
            s = chunk_s[q * STEP + k]
            both, more = sums[k]
            total[s, :, :BLK] += both[:, :BLK]
            total[s, :, BLK:] += both[:, BLK:] + more

    @pl.loop(0, steps[0])
    def _(q):
        fetch_step(q, lambda copy: copy.wait())
        step(q, left, low)

    for s in range(NNZ):
        at = 0 if s == 0 else KEPT - 1 + s if s < 3 else s - 2
        mid[at, 0] = low[s, :, :BLK].astype(jnp.bfloat16)
        mid[at, 1] = low[s, :, BLK:].astype(jnp.bfloat16)

    @pl.loop(0, steps[0])
    def _(q):
        step(q, mid, high)

    for s in range(NNZ):
        purified = 3.0 * low[s, :, :BLK] - 2.0 * high[s, :, :BLK]
        gradient = 3.0 * low[s, :, BLK:] - 2.0 * high[s, :, BLK:]
        x_ref[s] = purified
        g_ref[s] = gradient
        send_ref[0, s] = purified.astype(jnp.bfloat16)
        send_ref[1, s] = gradient.astype(jnp.bfloat16)


def one_row(name, steps, chunk_s, slots, places, mine, everything):
    f32, bf16 = jnp.float32, jnp.bfloat16
    vmem = pl.BlockSpec(memory_space=pltpu.VMEM)
    smem = pl.BlockSpec(memory_space=pltpu.SMEM)
    return pl.pallas_call(
        row_kernel,
        name=name,
        out_shape=(
            jax.ShapeDtypeStruct((NNZ, BLK, BLK), f32),
            jax.ShapeDtypeStruct((NNZ, BLK, BLK), f32),
            jax.ShapeDtypeStruct((2, NNZ, BLK, BLK), bf16),
        ),
        in_specs=[smem] * 5 + [pl.BlockSpec(memory_space=pl.ANY)],
        out_specs=(vmem, vmem, vmem),
        scratch_shapes=[
            pltpu.VMEM((NNZ + 1, 2, BLK, BLK), bf16),
            pltpu.VMEM((ENTRIES, 2, BLK, BLK), bf16),
            pltpu.VMEM((NNZ + 1, BLK, 2 * BLK), f32),
            pltpu.VMEM((NNZ + 1, BLK, 2 * BLK), f32),
            pltpu.VMEM((NNZ + 1, 2, BLK, BLK), bf16),
            pltpu.SemaphoreType.DMA((2,)),
            pltpu.SemaphoreType.DMA((ENTRIES,)),
        ],
        compiler_params=pltpu.CompilerParams(vmem_limit_bytes=40 << 20),
        cost_estimate=pl.CostEstimate(
            flops=2 * 2 * 3 * 104 * BLK**3, bytes_accessed=14 << 20, transcendentals=0
        ),
    )(steps, chunk_s, slots, places, mine, everything)


def tables(pattern, work_g, work_d):
    first = work_g * SPAN + work_d * 2
    cols = lax.dynamic_slice_in_dim(pattern, first, 2, 0)
    far = jnp.take(pattern, cols, axis=0)
    slot = jnp.arange(NNZ, dtype=jnp.int32)
    found = jnp.max(
        jnp.where(far[:, :, None, :] == cols[:, None, :, None], slot + 1, 0), axis=3
    ) - 1
    group, inner = cols // SPAN, cols % SPAN
    row = cols % 2
    inside = (group == work_g)[:, :, None]
    before = (group == (work_g + GROUPS - 1) % GROUPS)[:, :, None]
    short = jnp.clip(found, 0, 2)
    place = jnp.where(
        inside,
        jnp.where(
            (found == 1) | (found == 2),
            EXTRA + 2 * row[:, :, None] + jnp.clip(found - 1, 0, 1),
            inner[:, :, None] * KEPT + jnp.where(found < 3, 0, found - 2),
        ),
        EXTRA + 4 + 3 * row[:, :, None] + short + jnp.where(before, 0, 6),
    )
    hit = found >= 0
    held = hit.astype(jnp.int32)
    count = jnp.sum(held, axis=1)
    rank = jnp.sum(jnp.where(slot[None, :, None, None] > slot[None, None, :, None], held[:, None], 0), axis=2)
    chunks = (count + CHUNK - 1) // CHUNK
    start = jnp.sum(jnp.where(slot[None, None, :] < slot[None, :, None], chunks[:, None, :], 0), axis=2)
    spot = jnp.where(hit, start[:, None, :] * CHUNK + rank, -1).reshape(2, 1, NNZ * NNZ)
    chosen = spot == jnp.arange(ENTRIES, dtype=jnp.int32)[None, :, None]
    left_at = jnp.where(slot == 0, 0, jnp.where(slot < 3, KEPT - 1 + slot, slot - 2))
    both = jnp.broadcast_to(left_at[None, :, None] - NNZ, found.shape) + place * 32
    both = jnp.sum(jnp.where(chosen, both.reshape(2, 1, NNZ * NNZ) + NNZ, 0), axis=2)
    slots = jnp.where(jnp.any(chosen, axis=2), both % 32, NNZ)
    places = both // 32
    c = jnp.arange(ENTRIES // CHUNK, dtype=jnp.int32)[None, :, None]
    chunk_s = jnp.sum((c >= (start + chunks)[:, None, :]).astype(jnp.int32), axis=2)
    steps = (jnp.sum(chunks, axis=1, keepdims=True) + STEP - 1) // STEP
    return steps, chunk_s, slots, places


def on_device(pattern, density, hamiltonian):
    g, d = lax.axis_index("grp"), lax.axis_index("dom")
    y = d % 4
    own = g % 2 == y // 2
    work_g = jnp.where(own, g, g + 1 - 2 * (g % 2))
    work_d = jnp.where(own, d, d + 3 - 2 * y)
    lists = tables(pattern, work_g, work_d)
    everything = gather(density, hamiltonian)
    pairs = []
    for gg in range(8):
        for dd in range(16):
            yy = dd % 4
            if gg % 2 != yy // 2:
                pairs.append((gg * 16 + dd, (gg ^ 1) * 16 + dd + 3 - 2 * yy))
    mine, back = [], []
    for w in range(2):
        where = jnp.stack([(work_d * 2 + w) * KEPT, jnp.int32(EXTRA + 2 * w)])
        px, gx, out = one_row(f"row{w}", *(v[w] for v in lists), where, everything)
        mine.append((px, gx))
        back.append(lax.ppermute(out, ("grp", "dom"), pairs))
    res = []
    for k in range(2):
        res.append(jnp.stack([
            jnp.where(own, mine[w][k], back[w][k].astype(jnp.float32)) for w in range(2)
        ]))
    return tuple(res)


def solution(mesh):
    split = P(("grp", "dom"), None, None, None)
    return jax.shard_map(
        on_device,
        mesh=mesh,
        in_specs=(P(), split, split),
        out_specs=(split, split),
        check_vma=False,
    )
```

profile of v0, /device:TPU:1, one launch (start us, length us, event | category | flops | bytes accessed | tf_op | source)
XLA Modules:
  0.0 166.8 jit_solution(17434610015010238924)
XLA Ops:
  0.8 0.8 copy.17
  1.6 0.1 reshape.312
  1.7 0.6 gather_fusion
  2.3 0.1 broadcast_select_fusion
  2.4 0.7 select_reduce_fusion.2
  3.1 0.1 fusion.10
  3.2 0.1 select_reduce_fusion.3
  3.4 0.1 select_reduce_fusion.1
  3.5 0.1 select_n.206
  3.6 0.1 select_multiply_fusion
  3.7 0.1 reshape.309
  3.8 0.1 broadcast_in_dim.129
  3.8 0.1 broadcast_in_dim.130
  3.9 0.2 fusion.4
  4.1 0.1 select_reduce_fusion
  4.3 0.1 convert_reduce_fusion
  4.4 0.6 fusion.13
  5.0 0.1 pad_add_fusion.mine
  5.1 114.2 %gather.8.all_ref = bf16[464,2,128,128]{3,2,1,0:T(8,128)(2,1)} custom-call(bf16[2,16,128,128]{3,2,1,0:T(8,128)(2,1)} %p_ref.1, bf16[2,16,128,128]{3,2,1,0:T(8,128)(2,1)} %h_ref.1), custom_call_target="tpu_custom_call" | custom-call | tf_op jit(solution)/shard_map/gather/pallas_call | solution.py:266
  119.3 12.4 %row0.1 = (f32[16,128,128]{2,1,0:T(8,128)S(1)}, f32[16,128,128]{2,1,0:T(8,128)S(1)}, bf16[2,16,128,128]{3,2,1,0:T(8,128)(2,1)S(1)}) custom-call(s32[1]{0:T(128)} %bitcast.2.steps, s32[128]{0:T(128)S(1)} %get-tuple-element.33.chunk_s, s32[256]{0:T(256)S(1)} %bitcast.51, s32[256]{0:T(256)S(1)} %bitcast.52, s32[2]{0:T(128)S(1)} %pad_add_fusion.mine, ...), custom_call_target="tpu_custom_call" | custom-call | flops 2617245696 | bytes 14680064 | tf_op jit(solution)/shard_map/row0/pallas_call | solution.py:359
  131.7 1.9 %collective-permute-start = (bf16[2,16,128,128]{3,2,1,0:T(8,128)(2,1)S(1)}, bf16[2,16,128,128]{3,2,1,0:T(8,128)(2,1)}, u32[]{:S(2)}, u32[]{:S(2)}) collective-permute-start(bf16[2,16,128,128]{3,2,1,0:T(8,128)(2,1)S(1)} %get-tuple-element.9), channel_id=1, source_target_pairs={{2,17},{3,16},{6,21},{7,20},{10,25},{11,24},{14,29},{15,28},{16,3}... | collective-permute-start | bytes 3145736 | tf_op jit(solution)/shard_map/ppermute | solution.py:445
  133.6 0.1 pad_add_fusion.1.mine
  133.7 12.4 %row1.1 = (f32[16,128,128]{2,1,0:T(8,128)S(1)}, f32[16,128,128]{2,1,0:T(8,128)S(1)}, bf16[2,16,128,128]{3,2,1,0:T(8,128)(2,1)S(1)}) custom-call(s32[1]{0:T(128)} %bitcast.9.steps, s32[128]{0:T(128)S(1)} %get-tuple-element.34.chunk_s, s32[256]{0:T(256)S(1)} %bitcast.49, s32[256]{0:T(256)S(1)} %bitcast.50, s32[2]{0:T(128)S(1)} %pad_add_fusion.1.mine, ...), custom_call_target="tpu_custom_call" | custom-call | flops 2617245696 | bytes 14680064 | tf_op jit(solution)/shard_map/row1/pallas_call | solution.py:359
  146.1 4.9 %collective-permute-start.1 = (bf16[2,16,128,128]{3,2,1,0:T(8,128)(2,1)S(1)}, bf16[2,16,128,128]{3,2,1,0:T(8,128)(2,1)S(1)}, u32[]{:S(2)}, u32[]{:S(2)}) collective-permute-start(bf16[2,16,128,128]{3,2,1,0:T(8,128)(2,1)S(1)} %get-tuple-element.11), channel_id=1, source_target_pairs={{2,17},{3,16},{6,21},{7,20},{10,25},{11,24},{14,29},{15,28},{16,3}... | collective-permute-start | bytes 3145736 | tf_op jit(solution)/shard_map/ppermute | solution.py:445
  151.1 0.0 collective-permute-done
  151.1 1.5 fusion.1
  152.6 10.9 %collective-permute-done.1 = bf16[2,16,128,128]{3,2,1,0:T(8,128)(2,1)S(1)} collective-permute-done((bf16[2,16,128,128]{3,2,1,0:T(8,128)(2,1)S(1)}, bf16[2,16,128,128]{3,2,1,0:T(8,128)(2,1)S(1)}, u32[]{:S(2)}, u32[]{:S(2)}) %collective-permute-start.1) | collective-permute-done | bytes 1048608 | tf_op jit(solution)/shard_map/ppermute | solution.py:445
  163.5 0.3 fusion
  163.8 1.5 pad_maximum_fusion.1
  165.4 1.5 pad_maximum_fusion
  (19 shorter events, 0.2 us)
Async XLA Ops:
  131.7 19.4 %collective-permute-start = (bf16[2,16,128,128]{3,2,1,0:T(8,128)(2,1)S(1)}, bf16[2,16,128,128]{3,2,1,0:T(8,128)(2,1)}, u32[]{:S(2)}, u32[]{:S(2)}) collective-permute-start(bf16[2,16,128,128]{3,2,1,0:T(8,128)(2,1)S(1)} %get-tuple-element.9), channel_id=1, source_target_pairs={{2,17},{3,16},{6,21},{7,20},{10,25},{11,24},{14,29},{15,28},{16,3}... | collective-permute-start | bytes 3145736 | tf_op jit(solution)/shard_map/ppermute | solution.py:445
  146.1 17.4 %collective-permute-start.1 = (bf16[2,16,128,128]{3,2,1,0:T(8,128)(2,1)S(1)}, bf16[2,16,128,128]{3,2,1,0:T(8,128)(2,1)S(1)}, u32[]{:S(2)}, u32[]{:S(2)}) collective-permute-start(bf16[2,16,128,128]{3,2,1,0:T(8,128)(2,1)S(1)} %get-tuple-element.11), channel_id=1, source_target_pairs={{2,17},{3,16},{6,21},{7,20},{10,25},{11,24},{14,29},{15,28},{16,3}... | collective-permute-start | bytes 3145736 | tf_op jit(solution)/shard_map/ppermute | solution.py:445
where the time goes:
time: 167 us
  Pallas kernels  139 us (83%)
  waiting for transfers between devices  10.9 us (7%)
  starting transfers between devices  6.86 us (4%)
  other arithmetic  6.74 us (4%)
  local copies, waits for them, and re-layouts  2.39 us (1%)
    pallas_call x1, Pallas kernels, gather(): pl.pallas_call(gather_kernel, name='gather', out_shape=jax.ShapeDtypeStru...  114 us
    pallas_call x2, Pallas kernels, one_row(): pl.pallas_call(row_kernel, name=name, out_shape=(jax.ShapeDtypeStruct((NN...  24.8 us
    ppermute x2, waiting for transfers between devices, on_device(): back.append(lax.ppermute(out, ('grp', 'dom'), pairs))  10.9 us
    ppermute x2, starting transfers between devices, on_device(): back.append(lax.ppermute(out, ('grp', 'dom'), pairs))  6.86 us
    another operation x4, other arithmetic, on_device(): jnp.stack([jnp.where(own, mine[w][k], back[w][k].astype(jnp.float32)) for...  4.81 us
  transfers between devices with their start and end apart: 2, of which 1 were waited for; matrix products, arithmetic and copies ran while one was open for 1% of the time, Pallas kernels for 7%

commit v1 on v0

--- a/solution.py
+++ b/solution.py
@@ -15,46 +15,47 @@
 GROUPS = 8
 EXTRA = SPAN * KEPT
 TOTAL = EXTRA + 4 + 6 + 6
-CUT = 6
-ZH = CUT // 2
 CHUNK = 2
 STEP = 8
 ENTRIES = NNZ * NNZ
-YH = CUT + (KEPT - CUT) // 2
-PARTS = ((CUT + 2, NNZ, CUT), (0, 1, 0), (3, CUT + 2, 1))
+CUT = {"O": 5, "Q": 4}
+PARTS = ((CUT["Q"] + 2, NNZ, CUT["Q"]), (0, 1, 0), (3, CUT["Q"] + 2, 1))
 
 EVENTS = {
-    "Zp": ((0, CUT), 0, 0, "zp"),
-    "Zm": ((0, CUT), 0, 0, "zm"),
-    "ZpF": ((0, ZH), -1, 0, "zp"),
-    "ZmF": ((ZH, CUT), 1, 0, "zm"),
-    "ZY0": ((0, CUT), 0, 0, "y"),
-    "ZYm": ((0, CUT), -1, 0, "y"),
-    "ZYp": ((0, CUT), 1, 0, "y"),
-    "ZYa": ((0, ZH), 2, 0, "y"),
-    "ZYb": ((ZH, CUT), 2, 0, "y"),
-    "Y": ((CUT, KEPT), 0, 0, "y"),
-    "Yp": ((CUT, KEPT), 0, 0, "zp"),
-    "Ym": ((CUT, KEPT), 0, 0, "zm"),
-    "YpF": ((CUT, YH), -1, 0, "zp"),
-    "YmF": ((YH, KEPT), 1, 0, "zm"),
-    "Xp": ((CUT, KEPT), 0, 1, "zp"),
-    "Xm": ((CUT, KEPT), 0, 1, "zm"),
-    "XpF": ((CUT, YH), -1, 1, "zp"),
-    "XmF": ((YH, KEPT), 1, 1, "zm"),
+    "SZ": ("Z", "u", "v", "single"),
+    "PZ": ("Z", "u", "v", "pair"),
+    "FZ": ("Z", "u", "vs", "pair"),
+    "C0": ("Z", "u", "v", "cross"),
+    "Cs": ("Z", "u", "vs", "cross"),
+    "Cp": ("Z", "u", "vp", "cross"),
+    "Cf": ("Z", "u", "vf", "cross"),
+    "Y": ("Y", "u", "v", "cross"),
+    "SY": ("Y", "u", "v", "single"),
+    "FY": ("Y", "u", "vs", "pair"),
+    "SX": ("Y", "un", "v", "single"),
+    "FX": ("Y", "un", "vs", "pair"),
 }
-NAMES = tuple(EVENTS)
+DETOURS = {"PY": "u", "PX": "un"}
+NAMES = tuple(EVENTS) + tuple(n + h for n in DETOURS for h in "123")
 N_EV = len(NAMES)
+RELAY = {}
+LONG = TOTAL
+for _hop in "12":
+    for _name in DETOURS:
+        for _kind in "OQ":
+            RELAY[_name + _hop, _kind] = LONG
+            LONG += KEPT - CUT[_kind]
 ORDER = (
-    "R Zp O", "R Zm O", "S ZpF O", "S ZmF O", "R Y O", "S Xp O", "S Xm O", "QY",
-    "S Y Q", "S Yp Q", "S Ym Q", "S ZY0 O", "S ZYm O", "S ZYp O", "R Yp O", "R Ym O",
-    "S YpF O", "S YmF O", "QZ", "S Zp Q", "S Zm Q", "R Y Q", "S Xp Q", "S Xm Q",
-    "R ZpF O", "R ZmF O", "S ZYa O", "S ZYb O", "S ZY0 Q", "R Xp O", "R Xm O", "S XpF O",
-    "S XmF O", "R YpF O", "R YmF O", "R ZY0 O", "R Yp Q", "R Ym Q", "S YpF Q", "S YmF Q",
-    "R Zp Q", "R Zm Q", "S ZpF Q", "S ZmF Q", "S ZYm Q", "S ZYp Q", "R ZYm O", "R Xp Q",
-    "R Xm Q", "S XpF Q", "S XmF Q", "R ZpF Q", "R ZmF Q", "S ZYa Q", "S ZYb Q", "R ZYp O",
-    "R XpF O", "R XmF O", "R YpF Q", "R YmF Q", "R ZYa O", "R ZYb O", "R ZY0 Q", "R ZYm Q",
-    "R ZYp Q", "R XpF Q", "R XmF Q", "R ZYa Q", "R ZYb Q",
+    "R SZ O", "S FZ O", "R PZ O", "R PY1 O", "S PY2 O", "R Y O", "S SX O", "S PX1 O",
+    "QY", "S Y Q", "S SY Q", "S PY1 Q", "S C0 O", "S Cs O", "S Cp O",
+    "R FZ O", "S Cf O", "R PX1 O", "S PX2 O", "QZ", "S SZ Q", "S PZ Q",
+    "R SY O", "S FY O", "R PY2 O", "S PY3 O", "R PY1 Q", "S PY2 Q",
+    "R Y Q", "S SX Q", "S PX1 Q", "S C0 Q", "R SX O", "S FX O",
+    "R FY O", "R PX2 O", "S PX3 O", "R PX1 Q", "S PX2 Q", "R PY2 Q", "S PY3 Q",
+    "R SY Q", "S FY Q", "R SZ Q", "S FZ Q", "R PZ Q", "S Cs Q", "S Cp Q",
+    "R C0 O", "R Cs O", "R PX2 Q", "S PX3 Q", "R FX O", "R PY3 O", "R PX3 O", "R Cp O",
+    "R SX Q", "S FX Q", "R FZ Q", "S Cf Q", "R PY3 Q", "R Cf O",
+    "R FY Q", "R C0 Q", "R PX3 Q", "R Cs Q", "R Cp Q", "R FX Q", "R Cf Q",
 )
 
 
@@ -66,22 +67,43 @@
     g, d = lax.axis_index("grp"), lax.axis_index("dom")
     x, c = g // 2, g % 2
     z, y = d // 4, d % 4
-    host = y // 2
-    yn, yq = y + 1 - 2 * (y % 2), 3 - y
-    dq = z * 4 + yq
+    odd = x % 2
+    u, v = y + odd * (z - y), z + odd * (y - z)
+    host = u // 2
+    near = {"u": u, "un": u + 1 - 2 * (u % 2)}
+    far = v + 1 - 2 * (v % 2)
+    ring = {"v": v, "vs": far, "vp": 3 - v, "vf": (3 - v) + 1 - 2 * ((3 - v) % 2)}
+
+    def dom(uu, vv, swap=odd):
+        return vv * 4 + uu + swap * 3 * (uu - vv)
+
+    dq = dom(3 - u, v)
     sib_g = g + 1 - 2 * c
     sibling = (sib_g, d)
+    aside, back = (g + GROUPS + 2 - 4 * c) % GROUPS, (g + GROUPS - 2 + 4 * c) % GROUPS
     ways = {
-        "zp": (g, (z + 1) % 4 * 4 + y),
-        "zm": (g, (z + 3) % 4 * 4 + y),
-        "y": (g, z * 4 + yn),
+        "single": (g, dom(u, far)),
+        "pair": (g, dom(u, 3 - v)),
+        "cross": (g, dom(near["un"], v)),
+        "1": (aside, d),
+        "2": (g, dq),
+        "3": (back, d),
     }
     is_own = (c + host + 1) % 2
     work_g = is_own * g + (1 - is_own) * sib_g
     work_d = is_own * d + (1 - is_own) * dq
-    up, down = (g + 1) % GROUPS, (g + GROUPS - 1) % GROUPS
-    up_t = (is_own * (up + 1 - 2 * (up % 2)) + (1 - is_own) * up, is_own * dq + (1 - is_own) * d)
-    down_t = (is_own * (down + 1 - 2 * (down % 2)) + (1 - is_own) * down, is_own * dq + (1 - is_own) * d)
+
+    def worker(to):
+        turned = (to // 2) % 2
+        across = y + turned * (z - y)
+        same = (across // 2 + to + 1) % 2
+        there = d + (1 - turned) * (3 - 2 * y) + turned * 4 * (3 - 2 * z)
+        return (
+            same * to + (1 - same) * (to + 1 - 2 * (to % 2)),
+            same * d + (1 - same) * there,
+        )
+
+    up_t, down_t = worker((g + 1) % GROUPS), worker((g + GROUPS - 1) % GROUPS)
     partner_idle = (2 * x + host, dq)
 
     barrier = pltpu.get_barrier_semaphore()
@@ -90,7 +112,7 @@
         ((work_g + GROUPS - 1) % GROUPS, work_d), ((work_g + 1) % GROUPS, work_d),
     ):
         pl.semaphore_signal(barrier, inc=1, device_id=who, device_id_type=MESH)
-    pl.semaphore_wait(barrier, 8 - 2 * is_own)
+    pl.semaphore_wait(barrier, 11 - 2 * is_own)
 
     def at(dom, row, lo, n):
         return all_ref.at[pl.ds((dom * 2 + row) * KEPT + lo, n)]
@@ -162,23 +184,46 @@
             for copy in init_copies(core, "sibling"):
                 copy.wait_recv()
 
-    def dom_of(zz, col, kind):
-        yy = y if col == 0 else yn
-        return (z + zz + 4) % 4 * 4 + (yy if kind == "O" else 3 - yy)
+    def turn(uu, kind):
+        return uu if kind == "O" else 3 - uu
+
+    seen_by = {
+        "single": {"v": "vs"},
+        "pair": {"v": "vp", "vs": "vf"},
+        "cross": {"v": "v", "vs": "vs", "vp": "vp", "vf": "vf"},
+    }
 
     def event(name, kind, side):
-        (lo, hi), zz, col, way = EVENTS[name]
         k = NAMES.index(name) + (N_EV if kind == "Q" else 0)
-        if side == "R":
-            if way == "zp":
-                zz -= 1
-            elif way == "zm":
-                zz += 1
+        cut = CUT[kind]
+        n = KEPT - cut
+        if name in EVENTS:
+            part, col, place, way = EVENTS[name]
+            if side == "R":
+                place = seen_by[way][place]
+                if way == "cross":
+                    col = "un"
+            lo, n = (0, cut) if part == "Z" else (cut, n)
+            owner = dom(turn(near[col], kind), ring[place])
+            src = dst = at(owner, c, lo, n)
+            what = (owner, lo, n, k)
+        else:
+            way, base = name[2], name[:2]
+            col = DETOURS[base]
+            what = None
+            relay = {h: all_ref.at[pl.ds(RELAY[base + h, kind], n)] for h in "12"}
+            if way == "3" and side == "R":
+                owner = dom(turn(near[col], kind), 3 - v)
+                src = dst = at(owner, c, cut, n)
+                what = (owner, cut, n, k)
+            elif way == "3":
+                owner = dom(turn({"u": v, "un": far}[col], kind), 3 - u, 1 - odd)
+                src, dst = relay["2"], at(owner, c, cut, n)
+            elif way == "2":
+                src, dst = relay["1"], relay["2"]
             else:
-                col = 1
-        dom = dom_of(zz, col, kind)
-        ref = at(dom, c, lo, hi - lo)
-        return remote(ref, ref, ss.at[k], rs.at[k], ways[way]), (dom, lo, hi - lo, k)
+                src, dst = at(dom(turn(near[col], kind), v), c, cut, n), relay["1"]
+        return remote(src, dst, ss.at[k], rs.at[k], ways[way]), what
 
     passed = []
 
@@ -197,7 +242,8 @@
     def receive(name, kind):
         copy, what = event(name, kind, "R")
         copy.wait_recv()
-        to_sibling(*what)
+        if what is not None:
+            to_sibling(*what)
 
     def receive_partner(parts, lo, n, k):
         for part in parts:
@@ -207,7 +253,7 @@
                 remote(ref, ref, qs.at[0, part, a], qr.at[part, a], sibling).wait_recv()
         to_sibling(dq, lo, n, k)
 
-    for name in ("Y", "Zp", "Zm", "Yp", "Ym"):
+    for name in ("Y", "SZ", "PZ", "SY", "PY1"):
         send(name, "O")
 
     sides = side_copies()
@@ -226,9 +272,9 @@
 
     for step in ORDER:
         if step == "QY":
-            receive_partner((0,), CUT, KEPT - CUT, 2 * N_EV)
+            receive_partner((0,), CUT["Q"], KEPT - CUT["Q"], 2 * N_EV)
         elif step == "QZ":
-            receive_partner((1, 2), 0, CUT, 2 * N_EV + 1)
+            receive_partner((1, 2), 0, CUT["Q"], 2 * N_EV + 1)
         else:
             what, name, kind = step.split()
             (send if what == "S" else receive)(name, kind)
@@ -266,7 +312,7 @@
     return pl.pallas_call(
         gather_kernel,
         name="gather",
-        out_shape=jax.ShapeDtypeStruct((TOTAL, 2, BLK, BLK), jnp.bfloat16),
+        out_shape=jax.ShapeDtypeStruct((LONG, 2, BLK, BLK), jnp.bfloat16),
         in_specs=[pl.BlockSpec(memory_space=pl.ANY)] * 2,
         out_specs=pl.BlockSpec(memory_space=pl.ANY),
         scratch_shapes=[
@@ -425,18 +471,19 @@
 
 def on_device(pattern, density, hamiltonian):
     g, d = lax.axis_index("grp"), lax.axis_index("dom")
-    y = d % 4
-    own = g % 2 == y // 2
+    odd = g // 2 % 2
+    u = jnp.where(odd == 1, d // 4, d % 4)
+    own = g % 2 == u // 2
     work_g = jnp.where(own, g, g + 1 - 2 * (g % 2))
-    work_d = jnp.where(own, d, d + 3 - 2 * y)
+    work_d = jnp.where(own, d, d + jnp.where(odd == 1, 4, 1) * (3 - 2 * u))
     lists = tables(pattern, work_g, work_d)
     everything = gather(density, hamiltonian)
     pairs = []
     for gg in range(8):
         for dd in range(16):
-            yy = dd % 4
-            if gg % 2 != yy // 2:
-                pairs.append((gg * 16 + dd, (gg ^ 1) * 16 + dd + 3 - 2 * yy))
+            uu, unit = (dd // 4, 4) if gg // 2 % 2 else (dd % 4, 1)
+            if gg % 2 != uu // 2:
+                pairs.append((gg * 16 + dd, (gg ^ 1) * 16 + dd + unit * (3 - 2 * uu)))
     mine, back = [], []
     for w in range(2):
         where = jnp.stack([(work_d * 2 + w) * KEPT, jnp.int32(EXTRA + 2 * w)])

time: 167 us -> 181 us (1.084)
  Pallas kernels: 139 us -> 151 us
    pallas_call x1, Pallas kernels: 114 us -> 126 us  [gather(): pl.pallas_call(gather_kernel, name='gather', out_shape=jax.ShapeDtypeStru...]
where the time goes in v1:
time: 181 us; the launch traced here: 180 us
  Pallas kernels  151 us (83%)
  waiting for transfers between devices  12.6 us (7%)
  other arithmetic  6.74 us (4%)
  starting transfers between devices  6.61 us (4%)
  local copies, waits for them, and re-layouts  2.39 us (1%)
    pallas_call x1, Pallas kernels, gather(): pl.pallas_call(gather_kernel, name='gather', out_shape=jax.ShapeDtypeStru...  126 us
    pallas_call x2, Pallas kernels, one_row(): pl.pallas_call(row_kernel, name=name, out_shape=(jax.ShapeDtypeStruct((NN...  24.6 us
    ppermute x2, waiting for transfers between devices, on_device(): back.append(lax.ppermute(out, ('grp', 'dom'), pairs))  12.6 us
    ppermute x2, starting transfers between devices, on_device(): back.append(lax.ppermute(out, ('grp', 'dom'), pairs))  6.61 us
    another operation x4, other arithmetic, on_device(): jnp.stack([jnp.where(own, mine[w][k], back[w][k].astype(jnp.float32)) for...  4.81 us
  transfers between devices with their start and end apart: 2, of which 1 were waited for; matrix products, arithmetic and copies ran while one was open for 1% of the time, Pallas kernels for 7%

profile of v1, /device:TPU:1, one launch (start us, length us, event | category | flops | bytes accessed | tf_op | source)
XLA Modules:
  0.0 180.2 jit_solution(438119868016141141)
XLA Ops:
  0.8 0.8 copy.17
  1.7 0.1 reshape.312
  1.8 0.6 gather_fusion
  2.4 0.1 broadcast_select_fusion
  2.4 0.7 select_reduce_fusion.2
  3.2 0.1 fusion.10
  3.3 0.1 select_reduce_fusion.3
  3.4 0.1 select_reduce_fusion.1
  3.6 0.1 select_n.228
  3.6 0.1 select_multiply_fusion
  3.7 0.1 reshape.309
  3.8 0.1 broadcast_in_dim.129
  3.9 0.1 broadcast_in_dim.130
  4.0 0.2 fusion.4
  4.2 0.1 select_reduce_fusion
  4.4 0.1 convert_reduce_fusion
  4.5 0.6 fusion.13
  5.1 0.1 pad_add_fusion.mine
  5.1 126.3 %gather.8.all_ref = bf16[540,2,128,128]{3,2,1,0:T(8,128)(2,1)} custom-call(bf16[2,16,128,128]{3,2,1,0:T(8,128)(2,1)} %p_ref.1, bf16[2,16,128,128]{3,2,1,0:T(8,128)(2,1)} %h_ref.1), custom_call_target="tpu_custom_call" | custom-call | tf_op jit(solution)/shard_map/gather/pallas_call | solution.py:312
  131.5 12.1 %row0.1 = (f32[16,128,128]{2,1,0:T(8,128)S(1)}, f32[16,128,128]{2,1,0:T(8,128)S(1)}, bf16[2,16,128,128]{3,2,1,0:T(8,128)(2,1)S(1)}) custom-call(s32[1]{0:T(128)} %bitcast.2.steps, s32[128]{0:T(128)S(1)} %get-tuple-element.33.chunk_s, s32[256]{0:T(256)S(1)} %bitcast.51, s32[256]{0:T(256)S(1)} %bitcast.52, s32[2]{0:T(128)S(1)} %pad_add_fusion.mine, ...), custom_call_target="tpu_custom_call" | custom-call | flops 2617245696 | bytes 14680064 | tf_op jit(solution)/shard_map/row0/pallas_call | solution.py:405
  143.6 3.4 %collective-permute-start = (bf16[2,16,128,128]{3,2,1,0:T(8,128)(2,1)S(1)}, bf16[2,16,128,128]{3,2,1,0:T(8,128)(2,1)}, u32[]{:S(2)}, u32[]{:S(2)}) collective-permute-start(bf16[2,16,128,128]{3,2,1,0:T(8,128)(2,1)S(1)} %get-tuple-element.9), channel_id=1, source_target_pairs={{2,17},{3,16},{6,21},{7,20},{10,25},{11,24},{14,29},{15,28},{16,3}... | collective-permute-start | bytes 3145736 | tf_op jit(solution)/shard_map/ppermute | solution.py:492
  147.0 0.1 pad_add_fusion.1.mine
  147.1 12.5 %row1.1 = (f32[16,128,128]{2,1,0:T(8,128)S(1)}, f32[16,128,128]{2,1,0:T(8,128)S(1)}, bf16[2,16,128,128]{3,2,1,0:T(8,128)(2,1)S(1)}) custom-call(s32[1]{0:T(128)} %bitcast.9.steps, s32[128]{0:T(128)S(1)} %get-tuple-element.34.chunk_s, s32[256]{0:T(256)S(1)} %bitcast.49, s32[256]{0:T(256)S(1)} %bitcast.50, s32[2]{0:T(128)S(1)} %pad_add_fusion.1.mine, ...), custom_call_target="tpu_custom_call" | custom-call | flops 2617245696 | bytes 14680064 | tf_op jit(solution)/shard_map/row1/pallas_call | solution.py:405
  159.6 3.2 %collective-permute-start.1 = (bf16[2,16,128,128]{3,2,1,0:T(8,128)(2,1)S(1)}, bf16[2,16,128,128]{3,2,1,0:T(8,128)(2,1)S(1)}, u32[]{:S(2)}, u32[]{:S(2)}) collective-permute-start(bf16[2,16,128,128]{3,2,1,0:T(8,128)(2,1)S(1)} %get-tuple-element.11), channel_id=1, source_target_pairs={{2,17},{3,16},{6,21},{7,20},{10,25},{11,24},{14,29},{15,28},{16,3}... | collective-permute-start | bytes 3145736 | tf_op jit(solution)/shard_map/ppermute | solution.py:492
  162.8 0.0 collective-permute-done
  162.8 1.5 fusion.1
  164.3 12.6 %collective-permute-done.1 = bf16[2,16,128,128]{3,2,1,0:T(8,128)(2,1)S(1)} collective-permute-done((bf16[2,16,128,128]{3,2,1,0:T(8,128)(2,1)S(1)}, bf16[2,16,128,128]{3,2,1,0:T(8,128)(2,1)S(1)}, u32[]{:S(2)}, u32[]{:S(2)}) %collective-permute-start.1) | collective-permute-done | bytes 1048608 | tf_op jit(solution)/shard_map/ppermute | solution.py:492
  176.9 0.3 fusion
  177.2 1.5 pad_maximum_fusion.1
  178.8 1.5 pad_maximum_fusion
  (19 shorter events, 0.2 us)
Async XLA Ops:
  143.6 19.2 %collective-permute-start = (bf16[2,16,128,128]{3,2,1,0:T(8,128)(2,1)S(1)}, bf16[2,16,128,128]{3,2,1,0:T(8,128)(2,1)}, u32[]{:S(2)}, u32[]{:S(2)}) collective-permute-start(bf16[2,16,128,128]{3,2,1,0:T(8,128)(2,1)S(1)} %get-tuple-element.9), channel_id=1, source_target_pairs={{2,17},{3,16},{6,21},{7,20},{10,25},{11,24},{14,29},{15,28},{16,3}... | collective-permute-start | bytes 3145736 | tf_op jit(solution)/shard_map/ppermute | solution.py:492
  159.6 17.3 %collective-permute-start.1 = (bf16[2,16,128,128]{3,2,1,0:T(8,128)(2,1)S(1)}, bf16[2,16,128,128]{3,2,1,0:T(8,128)(2,1)S(1)}, u32[]{:S(2)}, u32[]{:S(2)}) collective-permute-start(bf16[2,16,128,128]{3,2,1,0:T(8,128)(2,1)S(1)} %get-tuple-element.11), channel_id=1, source_target_pairs={{2,17},{3,16},{6,21},{7,20},{10,25},{11,24},{14,29},{15,28},{16,3}... | collective-permute-start | bytes 3145736 | tf_op jit(solution)/shard_map/ppermute | solution.py:492

commit v2 on v1

--- a/solution.py
+++ b/solution.py
@@ -18,7 +18,7 @@
 CHUNK = 2
 STEP = 8
 ENTRIES = NNZ * NNZ
-CUT = {"O": 5, "Q": 4}
+CUT = {"O": 6, "Q": 4}
 PARTS = ((CUT["Q"] + 2, NNZ, CUT["Q"]), (0, 1, 0), (3, CUT["Q"] + 2, 1))
 
 EVENTS = {
@@ -46,16 +46,16 @@
             RELAY[_name + _hop, _kind] = LONG
             LONG += KEPT - CUT[_kind]
 ORDER = (
-    "R SZ O", "S FZ O", "R PZ O", "R PY1 O", "S PY2 O", "R Y O", "S SX O", "S PX1 O",
-    "QY", "S Y Q", "S SY Q", "S PY1 Q", "S C0 O", "S Cs O", "S Cp O",
-    "R FZ O", "S Cf O", "R PX1 O", "S PX2 O", "QZ", "S SZ Q", "S PZ Q",
-    "R SY O", "S FY O", "R PY2 O", "S PY3 O", "R PY1 Q", "S PY2 Q",
-    "R Y Q", "S SX Q", "S PX1 Q", "S C0 Q", "R SX O", "S FX O",
-    "R FY O", "R PX2 O", "S PX3 O", "R PX1 Q", "S PX2 Q", "R PY2 Q", "S PY3 Q",
-    "R SY Q", "S FY Q", "R SZ Q", "S FZ Q", "R PZ Q", "S Cs Q", "S Cp Q",
-    "R C0 O", "R Cs O", "R PX2 Q", "S PX3 Q", "R FX O", "R PY3 O", "R PX3 O", "R Cp O",
-    "R SX Q", "S FX Q", "R FZ Q", "S Cf Q", "R PY3 Q", "R Cf O",
-    "R FY Q", "R C0 Q", "R PX3 Q", "R Cs Q", "R Cp Q", "R FX Q", "R Cf Q",
+    "S SY O", "S Y O", "S PY1 O", "S PZ O", "S C0 O", "R SY O", "S SZ O", "S FY O",
+    "QY", "QZ", "R PY1 O", "S SZ Q", "S PY1 Q", "S Y Q", "S PY2 O", "R SZ O",
+    "S PZ Q", "R Y O", "S SY Q", "S FZ O", "R PY1 Q", "R SZ Q", "S C0 Q", "S FZ Q",
+    "S PY2 Q", "S PX1 O", "R Y Q", "S SX O", "S Cs Q", "R PZ O", "S Cs O", "R SY Q",
+    "S FY Q", "S PX1 Q", "R C0 Q", "R PX1 O", "S PX2 O", "R PZ Q", "S Cp O", "R SX O",
+    "R PY2 O", "R FY O", "R PY2 Q", "S Cp Q", "S PY3 O", "S SX Q", "S PY3 Q", "R Cs Q",
+    "R FZ O", "R PX1 Q", "S PX2 Q", "S FX O", "R PX2 O", "R SX Q", "S Cf O", "S FX Q",
+    "R FZ Q", "R Cp O", "R Cs O", "S PX3 O", "R PY3 Q", "SIDES", "S Cf Q", "R PX2 Q",
+    "S PX3 Q", "R FX Q", "R PX3 Q", "R C0 O", "R PY3 O", "R Cf Q", "R FX O", "R Cf O",
+    "R PX3 O", "R FY Q", "R Cp Q",
 )
 
 
@@ -253,25 +253,26 @@
                 remote(ref, ref, qs.at[0, part, a], qr.at[part, a], sibling).wait_recv()
         to_sibling(dq, lo, n, k)
 
-    for name in ("Y", "SZ", "PZ", "SY", "PY1"):
-        send(name, "O")
-
     sides = side_copies()
-    for copy in sides:
-        copy.start()
-
-    @pl.when(own)
-    def _():
-        for copy in extra_copies("own"):
+
+    def start_sides():
+        for copy in sides:
             copy.start()
 
-    @pl.when(jnp.logical_not(own))
-    def _():
-        for copy in extra_copies("partner"):
-            copy.start()
+        @pl.when(own)
+        def _():
+            for copy in extra_copies("own"):
+                copy.start()
+
+        @pl.when(jnp.logical_not(own))
+        def _():
+            for copy in extra_copies("partner"):
+                copy.start()
 
     for step in ORDER:
-        if step == "QY":
+        if step == "SIDES":
+            start_sides()
+        elif step == "QY":
             receive_partner((0,), CUT["Q"], KEPT - CUT["Q"], 2 * N_EV)
         elif step == "QZ":
             receive_partner((1, 2), 0, CUT["Q"], 2 * N_EV + 1)
@@ -324,10 +325,11 @@
     )(density, hamiltonian)
 
 
-def row_kernel(
-    steps, chunk_s, slots, places, mine, all_ref, x_ref, g_ref, send_ref,
-    left, right, low, high, mid, sem_a, sem_b,
-):
+def row_kernel(w, *refs):
+    steps, chunk_s, slots, places, mine, all_ref = refs[:6]
+    x_ref, g_ref, send_ref = refs[6 + 2 * w : 9 + 2 * w]
+    left, right, low, high, mid, full, short, sem_a, sem_b, sem_o = refs[9 + 2 * w :]
+
     def fetch_left(lo, n, at):
         return pltpu.make_async_copy(
             all_ref.at[pl.ds(at, n)], left.at[pl.ds(lo, n)], sem_a.at[lo // KEPT]
@@ -389,43 +391,107 @@
     def _(q):
         step(q, mid, high)
 
-    for s in range(NNZ):
-        purified = 3.0 * low[s, :, :BLK] - 2.0 * high[s, :, :BLK]
-        gradient = 3.0 * low[s, :, BLK:] - 2.0 * high[s, :, BLK:]
-        x_ref[s] = purified
-        g_ref[s] = gradient
-        send_ref[0, s] = purified.astype(jnp.bfloat16)
-        send_ref[1, s] = gradient.astype(jnp.bfloat16)
-
-
-def one_row(name, steps, chunk_s, slots, places, mine, everything):
+    def finished(keep):
+        out = []
+        for s in range(NNZ):
+            for k, ref in enumerate((x_ref, g_ref)):
+                part = pl.ds(k * BLK, BLK)
+                value = 3.0 * low[s, :, part] - 2.0 * high[s, :, part]
+                if keep:
+                    full[k, s] = value
+                else:
+                    short[k, s] = value.astype(jnp.bfloat16)
+                if s % 4 == 3:
+                    some = pl.ds(s - 3, 4)
+                    sem = sem_o.at[k, s // 4]
+                    out.append(
+                        pltpu.make_async_copy(full.at[k, some], ref.at[w, some], sem)
+                        if keep
+                        else pltpu.make_async_copy(short.at[k, some], send_ref.at[k, some], sem)
+                    )
+                    out[-1].start()
+        for copy in out:
+            copy.wait()
+
+    pl.when(mine[2] == 1)(lambda: finished(True))
+    pl.when(mine[2] == 0)(lambda: finished(False))
+
+
+WHOLE = jax.ShapeDtypeStruct((2, NNZ, BLK, BLK), jnp.float32)
+HALF = jax.ShapeDtypeStruct((2, NNZ, BLK, BLK), jnp.bfloat16)
+
+
+def one_row(w, steps, chunk_s, slots, places, mine, everything, *before):
     f32, bf16 = jnp.float32, jnp.bfloat16
-    vmem = pl.BlockSpec(memory_space=pltpu.VMEM)
+    anywhere = pl.BlockSpec(memory_space=pl.ANY)
     smem = pl.BlockSpec(memory_space=pltpu.SMEM)
     return pl.pallas_call(
-        row_kernel,
-        name=name,
-        out_shape=(
-            jax.ShapeDtypeStruct((NNZ, BLK, BLK), f32),
-            jax.ShapeDtypeStruct((NNZ, BLK, BLK), f32),
-            jax.ShapeDtypeStruct((2, NNZ, BLK, BLK), bf16),
-        ),
-        in_specs=[smem] * 5 + [pl.BlockSpec(memory_space=pl.ANY)],
-        out_specs=(vmem, vmem, vmem),
+        functools.partial(row_kernel, w),
+        name=f"row{w}",
+        out_shape=(WHOLE, WHOLE, HALF),
+        in_specs=[smem] * 5 + [anywhere] * (1 + len(before)),
+        out_specs=(anywhere,) * 3,
+        input_output_aliases={6 + k: k for k in range(len(before))},
         scratch_shapes=[
             pltpu.VMEM((NNZ + 1, 2, BLK, BLK), bf16),
             pltpu.VMEM((ENTRIES, 2, BLK, BLK), bf16),
             pltpu.VMEM((NNZ + 1, BLK, 2 * BLK), f32),
             pltpu.VMEM((NNZ + 1, BLK, 2 * BLK), f32),
             pltpu.VMEM((NNZ + 1, 2, BLK, BLK), bf16),
+            pltpu.VMEM((2, NNZ, BLK, BLK), f32),
+            pltpu.VMEM((2, NNZ, BLK, BLK), bf16),
             pltpu.SemaphoreType.DMA((2,)),
             pltpu.SemaphoreType.DMA((ENTRIES,)),
+            pltpu.SemaphoreType.DMA((2, 4)),
         ],
         compiler_params=pltpu.CompilerParams(vmem_limit_bytes=40 << 20),
         cost_estimate=pl.CostEstimate(
             flops=2 * 2 * 3 * 104 * BLK**3, bytes_accessed=14 << 20, transcendentals=0
         ),
-    )(steps, chunk_s, slots, places, mine, everything)
+    )(steps, chunk_s, slots, places, mine, everything, *before)
+
+
+def finish_kernel(w, mine, back, x_in, g_in, x_ref, g_ref, short, full, sem_i, sem_o):
+    @pl.when(mine[2] == 0)
+    def _():
+        def load(k, q):
+            some = pl.ds(4 * q, 4)
+            return pltpu.make_async_copy(back.at[k, some], short.at[k, some], sem_i.at[k, q])
+
+        def store(k, q):
+            some = pl.ds(4 * q, 4)
+            ref = (x_ref, g_ref)[k]
+            return pltpu.make_async_copy(full.at[k, some], ref.at[w, some], sem_o.at[k, q])
+
+        parts = [(k, q) for k in range(2) for q in range(4)]
+        for part in parts:
+            load(*part).start()
+        for k, q in parts:
+            load(k, q).wait()
+            full[k, 4 * q : 4 * q + 4] = short[k, 4 * q : 4 * q + 4].astype(jnp.float32)
+            store(k, q).start()
+        for part in parts:
+            store(*part).wait()
+
+
+def finish(w, mine, back, x, g):
+    anywhere = pl.BlockSpec(memory_space=pl.ANY)
+    return pl.pallas_call(
+        functools.partial(finish_kernel, w),
+        name=f"finish{w}",
+        out_shape=(WHOLE, WHOLE),
+        in_specs=[pl.BlockSpec(memory_space=pltpu.SMEM)] + [anywhere] * 3,
+        out_specs=(anywhere,) * 2,
+        input_output_aliases={2: 0, 3: 1},
+        scratch_shapes=[
+            pltpu.VMEM((2, NNZ, BLK, BLK), jnp.bfloat16),
+            pltpu.VMEM((2, NNZ, BLK, BLK), jnp.float32),
+            pltpu.SemaphoreType.DMA((2, 4)),
+            pltpu.SemaphoreType.DMA((2, 4)),
+        ],
+        compiler_params=pltpu.CompilerParams(vmem_limit_bytes=16 << 20),
+        cost_estimate=pl.CostEstimate(flops=1 << 20, bytes_accessed=3 << 20, transcendentals=0),
+    )(mine, back, x, g)
 
 
 def tables(pattern, work_g, work_d):
@@ -484,18 +550,14 @@
             uu, unit = (dd // 4, 4) if gg // 2 % 2 else (dd % 4, 1)
             if gg % 2 != uu // 2:
                 pairs.append((gg * 16 + dd, (gg ^ 1) * 16 + dd + unit * (3 - 2 * uu)))
-    mine, back = [], []
+    outs, back, mine = (), [], []
     for w in range(2):
-        where = jnp.stack([(work_d * 2 + w) * KEPT, jnp.int32(EXTRA + 2 * w)])
-        px, gx, out = one_row(f"row{w}", *(v[w] for v in lists), where, everything)
-        mine.append((px, gx))
-        back.append(lax.ppermute(out, ("grp", "dom"), pairs))
-    res = []
-    for k in range(2):
-        res.append(jnp.stack([
-            jnp.where(own, mine[w][k], back[w][k].astype(jnp.float32)) for w in range(2)
-        ]))
-    return tuple(res)
+        mine.append(jnp.stack([(work_d * 2 + w) * KEPT, jnp.int32(EXTRA + 2 * w), own.astype(jnp.int32)]))
+        *outs, send = one_row(w, *(v[w] for v in lists), mine[w], everything, *outs)
+        back.append(lax.ppermute(send, ("grp", "dom"), pairs))
+    for w in range(2):
+        outs = finish(w, mine[w], back[w], *outs)
+    return tuple(outs)
 
 
 def solution(mesh):

time: 181 us -> 186 us (1.028)
  Pallas kernels: 151 us -> 163 us
  other arithmetic: 6.74 us -> 1.93 us
  waiting for transfers between devices: 12.6 us -> 9.09 us
    pallas_call x2 -> x4, Pallas kernels: 24.6 us -> 34.6 us  [the longest x2 27.9 us: one_row(): pl.pallas_call(functools.partial(row_kernel, w), name=f'row{w}', out_shap...]
    another operation x6 -> x2, other arithmetic: 4.96 us -> 0.16 us  [on_device(): jnp.stack([(work_d * 2 + w) * KEPT, jnp.int32(EXTRA + 2 * w), own.astype(...]
    ppermute x2, waiting for transfers between devices: 12.6 us -> 9.09 us  [on_device(): back.append(lax.ppermute(send, ('grp', 'dom'), pairs))]
    pallas_call x1, Pallas kernels: 126 us -> 129 us  [gather(): pl.pallas_call(gather_kernel, name='gather', out_shape=jax.ShapeDtypeStru...]
  transfers between devices with their start and end apart: 2 -> 2, of which waited for: 1 -> 1; matrix products, arithmetic and copies ran while one was open for 1% -> 0% of each run, Pallas kernels for 7% -> 9%
where the time goes in v2:
time: 186 us; the launch traced here: 185 us
  Pallas kernels  163 us (88%)
  waiting for transfers between devices  9.09 us (5%)
  starting transfers between devices  7.18 us (4%)
  local copies, waits for them, and re-layouts  2.46 us (1%)
  other arithmetic  1.93 us (1%)
    pallas_call x1, Pallas kernels, gather(): pl.pallas_call(gather_kernel, name='gather', out_shape=jax.ShapeDtypeStru...  129 us
    pallas_call x2, Pallas kernels, one_row(): pl.pallas_call(functools.partial(row_kernel, w), name=f'row{w}', out_shap...  27.9 us
    ppermute x2, waiting for transfers between devices, on_device(): back.append(lax.ppermute(send, ('grp', 'dom'), pairs))  9.09 us
    ppermute x2, starting transfers between devices, on_device(): back.append(lax.ppermute(send, ('grp', 'dom'), pairs))  7.18 us
    pallas_call x2, Pallas kernels, finish(): pl.pallas_call(functools.partial(finish_kernel, w), name=f'finish{w}', ou...  6.72 us
  transfers between devices with their start and end apart: 2, of which 1 were waited for; matrix products, arithmetic and copies ran while one was open for 0% of the time, Pallas kernels for 9%

profile of v2, /device:TPU:1, one launch (start us, length us, event | category | flops | bytes accessed | tf_op | source)
XLA Modules:
  0.0 184.8 jit_solution(15435030241312936890)
XLA Ops:
  0.8 0.1 broadcast_in_dim.129
  0.9 0.1 broadcast_in_dim.130
  1.0 0.8 copy.23
  1.8 0.1 reshape.301
  1.9 0.6 gather_fusion
  2.5 0.1 broadcast_select_fusion
  2.6 0.7 select_reduce_fusion.2
  3.3 0.1 select_multiply_fusion
  3.4 0.1 reshape.298
  3.5 0.1 fusion.6
  3.6 0.7 fusion.9
  4.3 0.1 select_reduce_fusion.3
  4.4 0.1 select_reduce_fusion.1
  4.6 0.1 select_n.207
  4.6 0.2 fusion
  4.8 0.1 select_reduce_fusion
  5.0 0.1 convert_reduce_fusion
  5.1 128.6 %gather.8.refs_5_ = bf16[536,2,128,128]{3,2,1,0:T(8,128)(2,1)} custom-call(bf16[2,16,128,128]{3,2,1,0:T(8,128)(2,1)} %p_ref.1, bf16[2,16,128,128]{3,2,1,0:T(8,128)(2,1)} %h_ref.1), custom_call_target="tpu_custom_call" | custom-call | tf_op jit(solution)/shard_map/gather/pallas_call | solution.py:313
  133.7 0.1 add_add_fusion.2.refs_4_.mine
  133.8 13.9 %row0.1 = (f32[2,16,128,128]{3,2,1,0:T(8,128)}, f32[2,16,128,128]{3,2,1,0:T(8,128)}, bf16[2,16,128,128]{3,2,1,0:T(8,128)(2,1)S(1)}) custom-call(s32[1]{0:T(128)} %bitcast.8.refs_0_, s32[128]{0:T(128)S(1)} %get-tuple-element.33.refs_1_, s32[256]{0:T(256)S(1)} %bitcast.25, s32[256]{0:T(256)S(1)} %bitcast.24, s32[3]{0:T(128)S(1)} %add_add_fusion.2.refs_4_.mine, ...), custom_call_target="tpu_custom_call" | custom-call | flops 2617245696 | bytes 14680064 | tf_op jit(solution)/shard_map/row0/pallas_call | solution.py:428
  147.7 1.9 %collective-permute-start.1 = (bf16[2,16,128,128]{3,2,1,0:T(8,128)(2,1)S(1)}, bf16[2,16,128,128]{3,2,1,0:T(8,128)(2,1)S(1)}, u32[]{:S(2)}, u32[]{:S(2)}) collective-permute-start(bf16[2,16,128,128]{3,2,1,0:T(8,128)(2,1)S(1)} %get-tuple-element.13), channel_id=1, source_target_pairs={{2,17},{3,16},{6,21},{7,20},{10,25},{11,24},{14,29},{15,28},{16,3}... | collective-permute-start | bytes 3145736 | tf_op jit(solution)/shard_map/ppermute | solution.py:557
  149.6 0.1 add_add_fusion.1.refs_4_.mine
  149.7 14.0 %row1.1 = (f32[2,16,128,128]{3,2,1,0:T(8,128)}, f32[2,16,128,128]{3,2,1,0:T(8,128)}, bf16[2,16,128,128]{3,2,1,0:T(8,128)(2,1)S(1)}) custom-call(s32[1]{0:T(128)} %bitcast.4.refs_0_, s32[128]{0:T(128)S(1)} %get-tuple-element.34.refs_1_, s32[256]{0:T(256)S(1)} %bitcast.23, s32[256]{0:T(256)S(1)} %bitcast.22, ...), custom_call_target="tpu_custom_call", output_to_operand_aliasing={{0}: (6, {}), {1}: (7, {})} | custom-call | flops 2617245696 | bytes 14680064 | tf_op jit(solution)/shard_map/row1/pallas_call | solution.py:428
  163.7 5.3 %collective-permute-start = (bf16[2,16,128,128]{3,2,1,0:T(8,128)(2,1)S(1)}, bf16[2,16,128,128]{3,2,1,0:T(8,128)(2,1)S(1)}, u32[]{:S(2)}, u32[]{:S(2)}) collective-permute-start(bf16[2,16,128,128]{3,2,1,0:T(8,128)(2,1)S(1)} %get-tuple-element.12), channel_id=1, source_target_pairs={{2,17},{3,16},{6,21},{7,20},{10,25},{11,24},{14,29},{15,28},{16,3}... | collective-permute-start | bytes 3145736 | tf_op jit(solution)/shard_map/ppermute | solution.py:557
  169.0 0.0 collective-permute-done.1.back
  169.0 3.4 %finish0.1 = (f32[2,16,128,128]{3,2,1,0:T(8,128)}, f32[2,16,128,128]{3,2,1,0:T(8,128)}) custom-call(s32[3]{0:T(128)S(1)} %add_add_fusion.2.refs_4_.mine, bf16[2,16,128,128]{3,2,1,0:T(8,128)(2,1)S(1)} %collective-permute-done.1.back, f32[2,16,128,128]{3,2,1,0:T(8,128)} %get-tuple-element.14.x_in, ...), custom_call_target="tpu_custom_call", output_to_operand_aliasing={{0}: (2, {}), {1}: (3, {})} | custom-call | flops 1048576 | bytes 3145728 | tf_op jit(solution)/shard_map/finish0/pallas_call | solution.py:479
  172.4 9.1 %collective-permute-done.back = bf16[2,16,128,128]{3,2,1,0:T(8,128)(2,1)S(1)} collective-permute-done((bf16[2,16,128,128]{3,2,1,0:T(8,128)(2,1)S(1)}, bf16[2,16,128,128]{3,2,1,0:T(8,128)(2,1)S(1)}, u32[]{:S(2)}, u32[]{:S(2)}) %collective-permute-start) | collective-permute-done | bytes 1048608 | tf_op jit(solution)/shard_map/ppermute | solution.py:557
  181.4 3.4 %finish1.1 = (f32[2,16,128,128]{3,2,1,0:T(8,128)}, f32[2,16,128,128]{3,2,1,0:T(8,128)}) custom-call(s32[3]{0:T(128)S(1)} %add_add_fusion.1.refs_4_.mine, bf16[2,16,128,128]{3,2,1,0:T(8,128)(2,1)S(1)} %collective-permute-done.back, f32[2,16,128,128]{3,2,1,0:T(8,128)} %get-tuple-element.16.x_in, ...), custom_call_target="tpu_custom_call", output_to_operand_aliasing={{0}: (2, {}), {1}: (3, {})} | custom-call | flops 1048576 | bytes 3145728 | tf_op jit(solution)/shard_map/finish1/pallas_call | solution.py:479
  (19 shorter events, 0.2 us)
Async XLA Ops:
  147.7 21.3 %collective-permute-start.1 = (bf16[2,16,128,128]{3,2,1,0:T(8,128)(2,1)S(1)}, bf16[2,16,128,128]{3,2,1,0:T(8,128)(2,1)S(1)}, u32[]{:S(2)}, u32[]{:S(2)}) collective-permute-start(bf16[2,16,128,128]{3,2,1,0:T(8,128)(2,1)S(1)} %get-tuple-element.13), channel_id=1, source_target_pairs={{2,17},{3,16},{6,21},{7,20},{10,25},{11,24},{14,29},{15,28},{16,3}... | collective-permute-start | bytes 3145736 | tf_op jit(solution)/shard_map/ppermute | solution.py:557
  163.7 17.7 %collective-permute-start = (bf16[2,16,128,128]{3,2,1,0:T(8,128)(2,1)S(1)}, bf16[2,16,128,128]{3,2,1,0:T(8,128)(2,1)S(1)}, u32[]{:S(2)}, u32[]{:S(2)}) collective-permute-start(bf16[2,16,128,128]{3,2,1,0:T(8,128)(2,1)S(1)} %get-tuple-element.12), channel_id=1, source_target_pairs={{2,17},{3,16},{6,21},{7,20},{10,25},{11,24},{14,29},{15,28},{16,3}... | collective-permute-start | bytes 3145736 | tf_op jit(solution)/shard_map/ppermute | solution.py:557

commit v3 on v1

--- a/solution.py
+++ b/solution.py
@@ -18,7 +18,7 @@
 CHUNK = 2
 STEP = 8
 ENTRIES = NNZ * NNZ
-CUT = {"O": 5, "Q": 4}
+CUT = {"O": 7, "Q": 4}
 PARTS = ((CUT["Q"] + 2, NNZ, CUT["Q"]), (0, 1, 0), (3, CUT["Q"] + 2, 1))
 
 EVENTS = {
@@ -46,16 +46,16 @@
             RELAY[_name + _hop, _kind] = LONG
             LONG += KEPT - CUT[_kind]
 ORDER = (
-    "R SZ O", "S FZ O", "R PZ O", "R PY1 O", "S PY2 O", "R Y O", "S SX O", "S PX1 O",
-    "QY", "S Y Q", "S SY Q", "S PY1 Q", "S C0 O", "S Cs O", "S Cp O",
-    "R FZ O", "S Cf O", "R PX1 O", "S PX2 O", "QZ", "S SZ Q", "S PZ Q",
-    "R SY O", "S FY O", "R PY2 O", "S PY3 O", "R PY1 Q", "S PY2 Q",
-    "R Y Q", "S SX Q", "S PX1 Q", "S C0 Q", "R SX O", "S FX O",
-    "R FY O", "R PX2 O", "S PX3 O", "R PX1 Q", "S PX2 Q", "R PY2 Q", "S PY3 Q",
-    "R SY Q", "S FY Q", "R SZ Q", "S FZ Q", "R PZ Q", "S Cs Q", "S Cp Q",
-    "R C0 O", "R Cs O", "R PX2 Q", "S PX3 Q", "R FX O", "R PY3 O", "R PX3 O", "R Cp O",
-    "R SX Q", "S FX Q", "R FZ Q", "S Cf Q", "R PY3 Q", "R Cf O",
-    "R FY Q", "R C0 Q", "R PX3 Q", "R Cs Q", "R Cp Q", "R FX Q", "R Cf Q",
+    "S Y O", "S PY1 O", "S C0 O", "S SZ O", "S PZ O", "R SZ O", "R PZ O", "S FZ O",
+    "S SY O", "QY", "S Y Q", "R SY O", "S SY Q", "R PY1 O", "R Y O", "QZ",
+    "S PY2 O", "S PX1 O", "S FY O", "S PY1 Q", "R PX1 O", "R C0 O", "S PX2 O", "S SX O",
+    "S Cp O", "S PZ Q", "R Y Q", "R SY Q", "R PY2 O", "S C0 Q", "S SZ Q", "R PY1 Q",
+    "S PY3 O", "R FZ O", "S PX1 Q", "S PY2 Q", "S FY Q", "S Cf O", "R PX2 O", "R FY O",
+    "S Cs O", "S PX3 O", "R PY3 O", "R SZ Q", "R SX O", "S Cs Q", "R PX1 Q", "S FZ Q",
+    "R FY Q", "S PX2 Q", "R PZ Q", "S FX O", "S SX Q", "R FZ Q", "R PY2 Q", "S PY3 Q",
+    "S Cf Q", "R SX Q", "S FX Q", "R Cf O", "R PX2 Q", "R FX O", "S PX3 Q", "R C0 Q",
+    "S Cp Q", "R PY3 Q", "SIDES", "R FX Q", "R Cf Q", "R PX3 O", "R Cs Q", "R Cs O",
+    "R Cp Q", "R Cp O", "R PX3 Q",
 )
 
 
@@ -153,12 +153,13 @@
 
     def side_copies():
         out = []
-        for k, who in enumerate((up_t, down_t)):
+        for k, who, parts in ((0, up_t, ((0, 1), (2, 1))), (1, down_t, ((0, 2),))):
             for row in range(2):
                 for a in range(2):
-                    src = args[a].at[row, pl.ds(0, 3)]
-                    dst = all_ref.at[pl.ds(EXTRA + 4 + 6 * k + 3 * row, 3), a]
-                    out.append(remote(src, dst, xs.at[k, row, a], xr.at[k, row, a], who))
+                    for q, (first, n) in enumerate(parts):
+                        src = args[a].at[row, pl.ds(first, n)]
+                        dst = all_ref.at[pl.ds(EXTRA + 4 + 6 * k + 3 * row + first, n), a]
+                        out.append(remote(src, dst, xs.at[2 * k + q, row, a], xr.at[2 * k + q, row, a], who))
         return out
 
     own = c == host
@@ -253,25 +254,26 @@
                 remote(ref, ref, qs.at[0, part, a], qr.at[part, a], sibling).wait_recv()
         to_sibling(dq, lo, n, k)
 
-    for name in ("Y", "SZ", "PZ", "SY", "PY1"):
-        send(name, "O")
-
     sides = side_copies()
-    for copy in sides:
-        copy.start()
-
-    @pl.when(own)
-    def _():
-        for copy in extra_copies("own"):
+
+    def start_sides():
+        for copy in sides:
             copy.start()
 
-    @pl.when(jnp.logical_not(own))
-    def _():
-        for copy in extra_copies("partner"):
-            copy.start()
+        @pl.when(own)
+        def _():
+            for copy in extra_copies("own"):
+                copy.start()
+
+        @pl.when(jnp.logical_not(own))
+        def _():
+            for copy in extra_copies("partner"):
+                copy.start()
 
     for step in ORDER:
-        if step == "QY":
+        if step == "SIDES":
+            start_sides()
+        elif step == "QY":
             receive_partner((0,), CUT["Q"], KEPT - CUT["Q"], 2 * N_EV)
         elif step == "QZ":
             receive_partner((1, 2), 0, CUT["Q"], 2 * N_EV + 1)
@@ -313,12 +315,12 @@
         gather_kernel,
         name="gather",
         out_shape=jax.ShapeDtypeStruct((LONG, 2, BLK, BLK), jnp.bfloat16),
-        in_specs=[pl.BlockSpec(memory_space=pl.ANY)] * 2,
+        in_specs=[pl.BlockSpec(memory_space=pltpu.VMEM)] * 2,
         out_specs=pl.BlockSpec(memory_space=pl.ANY),
         scratch_shapes=[
             dma((2 * N_EV,)), dma((2 * N_EV,)), dma((2 * N_EV + 2,)), dma((2 * N_EV + 2,)),
             dma((2, 3, 2)), dma((2, 3, 2)), dma((2, 3, 2)), dma((2, 3, 2)), dma((3, 2)),
-            dma((2, 2)), dma((2, 2)), dma((2, 2, 2)), dma((2, 2, 2)),
+            dma((2, 2)), dma((2, 2)), dma((3, 2, 2)), dma((3, 2, 2)),
         ],
         compiler_params=pltpu.CompilerParams(collective_id=0, has_side_effects=True),
     )(density, hamiltonian)

time: 181 us -> 162 us (0.90)
  Pallas kernels: 151 us -> 133 us
    pallas_call x1, Pallas kernels: 126 us -> 107 us  [gather(): pl.pallas_call(gather_kernel, name='gather', out_shape=jax.ShapeDtypeStru...]
  transfers between devices with their start and end apart: 2 -> 2, of which waited for: 1 -> 1; matrix products, arithmetic and copies ran while one was open for 1% -> 1% of each run, Pallas kernels for 7% -> 8%
where the time goes in v3:
time: 162 us
  Pallas kernels  133 us (82%)
  waiting for transfers between devices  10.9 us (7%)
  starting transfers between devices  7.73 us (5%)
  other arithmetic  6.74 us (4%)
  local copies, waits for them, and re-layouts  2.39 us (1%)
    pallas_call x1, Pallas kernels, gather(): pl.pallas_call(gather_kernel, name='gather', out_shape=jax.ShapeDtypeStru...  107 us
    pallas_call x2, Pallas kernels, one_row(): pl.pallas_call(row_kernel, name=name, out_shape=(jax.ShapeDtypeStruct((NN...  26.1 us
    ppermute x2, waiting for transfers between devices, on_device(): back.append(lax.ppermute(out, ('grp', 'dom'), pairs))  10.9 us
    ppermute x2, starting transfers between devices, on_device(): back.append(lax.ppermute(out, ('grp', 'dom'), pairs))  7.73 us
    another operation x4, other arithmetic, on_device(): jnp.stack([jnp.where(own, mine[w][k], back[w][k].astype(jnp.float32)) for...  4.81 us
  transfers between devices with their start and end apart: 2, of which 1 were waited for; matrix products, arithmetic and copies ran while one was open for 1% of the time, Pallas kernels for 8%

profile of v3, /device:TPU:1, one launch (start us, length us, event | category | flops | bytes accessed | tf_op | source)
XLA Modules:
  0.0 162.1 jit_solution(17897901026122244446)
XLA Ops:
  0.8 0.8 copy.17
  1.7 0.1 reshape.312
  1.8 0.6 gather_fusion
  2.4 0.1 broadcast_select_fusion
  2.4 0.7 select_reduce_fusion.2
  3.2 0.1 fusion.10
  3.3 0.1 select_reduce_fusion.3
  3.4 0.1 select_reduce_fusion.1
  3.6 0.1 select_n.228
  3.6 0.1 select_multiply_fusion
  3.7 0.1 reshape.309
  3.8 0.1 broadcast_in_dim.129
  3.9 0.1 broadcast_in_dim.130
  4.0 0.2 fusion.4
  4.2 0.1 select_reduce_fusion
  4.4 0.1 convert_reduce_fusion
  4.5 0.6 fusion.13
  5.1 0.1 pad_add_fusion.mine
  5.1 107.2 %gather.8.all_ref = bf16[532,2,128,128]{3,2,1,0:T(8,128)(2,1)} custom-call(bf16[2,16,128,128]{3,2,1,0:T(8,128)(2,1)} %p_ref.1, bf16[2,16,128,128]{3,2,1,0:T(8,128)(2,1)} %h_ref.1), custom_call_target="tpu_custom_call" | custom-call | tf_op jit(solution)/shard_map/gather/pallas_call | solution.py:314
  112.4 13.6 %row0.1 = (f32[16,128,128]{2,1,0:T(8,128)S(1)}, f32[16,128,128]{2,1,0:T(8,128)S(1)}, bf16[2,16,128,128]{3,2,1,0:T(8,128)(2,1)S(1)}) custom-call(s32[1]{0:T(128)} %bitcast.2.steps, s32[128]{0:T(128)S(1)} %get-tuple-element.33.chunk_s, s32[256]{0:T(256)S(1)} %bitcast.51, s32[256]{0:T(256)S(1)} %bitcast.52, s32[2]{0:T(128)S(1)} %pad_add_fusion.mine, ...), custom_call_target="tpu_custom_call" | custom-call | flops 2617245696 | bytes 14680064 | tf_op jit(solution)/shard_map/row0/pallas_call | solution.py:407
  125.9 1.9 %collective-permute-start = (bf16[2,16,128,128]{3,2,1,0:T(8,128)(2,1)S(1)}, bf16[2,16,128,128]{3,2,1,0:T(8,128)(2,1)}, u32[]{:S(2)}, u32[]{:S(2)}) collective-permute-start(bf16[2,16,128,128]{3,2,1,0:T(8,128)(2,1)S(1)} %get-tuple-element.9), channel_id=1, source_target_pairs={{2,17},{3,16},{6,21},{7,20},{10,25},{11,24},{14,29},{15,28},{16,3}... | collective-permute-start | bytes 3145736 | tf_op jit(solution)/shard_map/ppermute | solution.py:494
  127.9 0.1 pad_add_fusion.1.mine
  127.9 12.5 %row1.1 = (f32[16,128,128]{2,1,0:T(8,128)S(1)}, f32[16,128,128]{2,1,0:T(8,128)S(1)}, bf16[2,16,128,128]{3,2,1,0:T(8,128)(2,1)S(1)}) custom-call(s32[1]{0:T(128)} %bitcast.9.steps, s32[128]{0:T(128)S(1)} %get-tuple-element.34.chunk_s, s32[256]{0:T(256)S(1)} %bitcast.49, s32[256]{0:T(256)S(1)} %bitcast.50, s32[2]{0:T(128)S(1)} %pad_add_fusion.1.mine, ...), custom_call_target="tpu_custom_call" | custom-call | flops 2617245696 | bytes 14680064 | tf_op jit(solution)/shard_map/row1/pallas_call | solution.py:407
  140.5 5.8 %collective-permute-start.1 = (bf16[2,16,128,128]{3,2,1,0:T(8,128)(2,1)S(1)}, bf16[2,16,128,128]{3,2,1,0:T(8,128)(2,1)S(1)}, u32[]{:S(2)}, u32[]{:S(2)}) collective-permute-start(bf16[2,16,128,128]{3,2,1,0:T(8,128)(2,1)S(1)} %get-tuple-element.11), channel_id=1, source_target_pairs={{2,17},{3,16},{6,21},{7,20},{10,25},{11,24},{14,29},{15,28},{16,3}... | collective-permute-start | bytes 3145736 | tf_op jit(solution)/shard_map/ppermute | solution.py:494
  146.3 0.0 collective-permute-done
  146.3 1.5 fusion.1
  147.9 10.9 %collective-permute-done.1 = bf16[2,16,128,128]{3,2,1,0:T(8,128)(2,1)S(1)} collective-permute-done((bf16[2,16,128,128]{3,2,1,0:T(8,128)(2,1)S(1)}, bf16[2,16,128,128]{3,2,1,0:T(8,128)(2,1)S(1)}, u32[]{:S(2)}, u32[]{:S(2)}) %collective-permute-start.1) | collective-permute-done | bytes 1048608 | tf_op jit(solution)/shard_map/ppermute | solution.py:494
  158.8 0.3 fusion
  159.1 1.5 pad_maximum_fusion.1
  160.6 1.5 pad_maximum_fusion
  (19 shorter events, 0.2 us)
Async XLA Ops:
  125.9 20.4 %collective-permute-start = (bf16[2,16,128,128]{3,2,1,0:T(8,128)(2,1)S(1)}, bf16[2,16,128,128]{3,2,1,0:T(8,128)(2,1)}, u32[]{:S(2)}, u32[]{:S(2)}) collective-permute-start(bf16[2,16,128,128]{3,2,1,0:T(8,128)(2,1)S(1)} %get-tuple-element.9), channel_id=1, source_target_pairs={{2,17},{3,16},{6,21},{7,20},{10,25},{11,24},{14,29},{15,28},{16,3}... | collective-permute-start | bytes 3145736 | tf_op jit(solution)/shard_map/ppermute | solution.py:494
  140.5 18.3 %collective-permute-start.1 = (bf16[2,16,128,128]{3,2,1,0:T(8,128)(2,1)S(1)}, bf16[2,16,128,128]{3,2,1,0:T(8,128)(2,1)S(1)}, u32[]{:S(2)}, u32[]{:S(2)}) collective-permute-start(bf16[2,16,128,128]{3,2,1,0:T(8,128)(2,1)S(1)} %get-tuple-element.11), channel_id=1, source_target_pairs={{2,17},{3,16},{6,21},{7,20},{10,25},{11,24},{14,29},{15,28},{16,3}... | collective-permute-start | bytes 3145736 | tf_op jit(solution)/shard_map/ppermute | solution.py:494

commit v4 on v3

--- a/solution.py
+++ b/solution.py
@@ -18,6 +18,7 @@
 CHUNK = 2
 STEP = 8
 ENTRIES = NNZ * NNZ
+WHERE = 2 * ENTRIES + ENTRIES // CHUNK
 CUT = {"O": 7, "Q": 4}
 PARTS = ((CUT["Q"] + 2, NNZ, CUT["Q"]), (0, 1, 0), (3, CUT["Q"] + 2, 1))
 
@@ -327,7 +328,7 @@
 
 
 def row_kernel(
-    steps, chunk_s, slots, places, mine, all_ref, x_ref, g_ref, send_ref,
+    table, all_ref, x_ref, g_ref, send_ref,
     left, right, low, high, mid, sem_a, sem_b,
 ):
     def fetch_left(lo, n, at):
@@ -336,17 +337,17 @@
         )
 
     def fetch(e):
-        return pltpu.make_async_copy(all_ref.at[places[e]], right.at[e], sem_b.at[e])
+        return pltpu.make_async_copy(all_ref.at[table[e]], right.at[e], sem_b.at[e])
 
     def fetch_step(q, what):
         for k in range(STEP * CHUNK):
             what(fetch(q * (STEP * CHUNK) + k))
 
-    a_copies = (fetch_left(0, KEPT, mine[0]), fetch_left(KEPT, 2, mine[1]))
+    a_copies = (fetch_left(0, KEPT, table[WHERE]), fetch_left(KEPT, 2, table[WHERE + 1]))
     for copy in a_copies:
         copy.start()
 
-    @pl.loop(0, steps[0])
+    @pl.loop(0, table[WHERE + 2])
     def _(q):
         fetch_step(q, lambda copy: copy.start())
 
@@ -363,7 +364,7 @@
         for k in range(STEP):
             first = (q * STEP + k) * CHUNK
             e = [first + p for p in range(CHUNK)]
-            t = [slots[p] for p in e]
+            t = [table[ENTRIES + p] for p in e]
             a = jnp.concatenate([a_ref[p, 0] for p in t], axis=1)
             b = jnp.concatenate([a_ref[p, 1] for p in t], axis=1)
             den = jnp.concatenate([right[p, 0] for p in e], axis=0)
@@ -372,12 +373,12 @@
             more = jnp.dot(b, den, preferred_element_type=jnp.float32)
             sums.append((both, more))
         for k in range(STEP):
-            s = chunk_s[q * STEP + k]
+            s = table[2 * ENTRIES + q * STEP + k]
             both, more = sums[k]
             total[s, :, :BLK] += both[:, :BLK]
             total[s, :, BLK:] += both[:, BLK:] + more
 
-    @pl.loop(0, steps[0])
+    @pl.loop(0, table[WHERE + 2])
     def _(q):
         fetch_step(q, lambda copy: copy.wait())
         step(q, left, low)
@@ -387,7 +388,7 @@
         mid[at, 0] = low[s, :, :BLK].astype(jnp.bfloat16)
         mid[at, 1] = low[s, :, BLK:].astype(jnp.bfloat16)
 
-    @pl.loop(0, steps[0])
+    @pl.loop(0, table[WHERE + 2])
     def _(q):
         step(q, mid, high)
 
@@ -400,7 +401,7 @@
         send_ref[1, s] = gradient.astype(jnp.bfloat16)
 
 
-def one_row(name, steps, chunk_s, slots, places, mine, everything):
+def one_row(name, table, everything):
     f32, bf16 = jnp.float32, jnp.bfloat16
     vmem = pl.BlockSpec(memory_space=pltpu.VMEM)
     smem = pl.BlockSpec(memory_space=pltpu.SMEM)
@@ -412,7 +413,7 @@
             jax.ShapeDtypeStruct((NNZ, BLK, BLK), f32),
             jax.ShapeDtypeStruct((2, NNZ, BLK, BLK), bf16),
         ),
-        in_specs=[smem] * 5 + [pl.BlockSpec(memory_space=pl.ANY)],
+        in_specs=[smem, pl.BlockSpec(memory_space=pl.ANY)],
         out_specs=(vmem, vmem, vmem),
         scratch_shapes=[
             pltpu.VMEM((NNZ + 1, 2, BLK, BLK), bf16),
@@ -427,13 +428,15 @@
         cost_estimate=pl.CostEstimate(
             flops=2 * 2 * 3 * 104 * BLK**3, bytes_accessed=14 << 20, transcendentals=0
         ),
-    )(steps, chunk_s, slots, places, mine, everything)
+    )(table, everything)
 
 
 def tables(pattern, work_g, work_d):
     first = work_g * SPAN + work_d * 2
     cols = lax.dynamic_slice_in_dim(pattern, first, 2, 0)
-    far = jnp.take(pattern, cols, axis=0)
+    picks = (cols.reshape(2 * NNZ, 1) == jnp.arange(pattern.shape[0], dtype=jnp.int32)).astype(jnp.bfloat16)
+    far = jnp.dot(picks, pattern.astype(jnp.bfloat16), preferred_element_type=jnp.float32)
+    far = far.astype(jnp.int32).reshape(2, NNZ, NNZ)
     slot = jnp.arange(NNZ, dtype=jnp.int32)
     found = jnp.max(
         jnp.where(far[:, :, None, :] == cols[:, None, :, None], slot + 1, 0), axis=3
@@ -468,7 +471,9 @@
     c = jnp.arange(ENTRIES // CHUNK, dtype=jnp.int32)[None, :, None]
     chunk_s = jnp.sum((c >= (start + chunks)[:, None, :]).astype(jnp.int32), axis=2)
     steps = (jnp.sum(chunks, axis=1, keepdims=True) + STEP - 1) // STEP
-    return steps, chunk_s, slots, places
+    row_at = (work_d * 2 + jnp.arange(2, dtype=jnp.int32)[:, None]) * KEPT
+    extra_at = EXTRA + 2 * jnp.arange(2, dtype=jnp.int32)[:, None]
+    return jnp.concatenate([places, slots, chunk_s, row_at, extra_at, steps], axis=1)
 
 
 def on_device(pattern, density, hamiltonian):
@@ -488,15 +493,14 @@
                 pairs.append((gg * 16 + dd, (gg ^ 1) * 16 + dd + unit * (3 - 2 * uu)))
     mine, back = [], []
     for w in range(2):
-        where = jnp.stack([(work_d * 2 + w) * KEPT, jnp.int32(EXTRA + 2 * w)])
-        px, gx, out = one_row(f"row{w}", *(v[w] for v in lists), where, everything)
+        px, gx, out = one_row(f"row{w}", lists[w], everything)
         mine.append((px, gx))
         back.append(lax.ppermute(out, ("grp", "dom"), pairs))
     res = []
     for k in range(2):
-        res.append(jnp.stack([
-            jnp.where(own, mine[w][k], back[w][k].astype(jnp.float32)) for w in range(2)
-        ]))
+        rows = [jnp.where(own, mine[w][k], back[w][k].astype(jnp.float32))[None] for w in range(2)]
+        both = jnp.broadcast_to(rows[0], (2, NNZ, BLK, BLK))
+        res.append(lax.dynamic_update_slice(both, rows[1], (1, 0, 0, 0)))
     return tuple(res)
 
 

time: 162 us -> 159 us (0.981)
  other arithmetic: 6.74 us -> 2.22 us
  Pallas kernels: 133 us -> 131 us
    another operation x6 -> x0, other arithmetic: 4.96 us -> none  [the longest x4 4.81 us: on_device(): jnp.stack([jnp.where(own, mine[w][k], back[w][k].astype(jnp.float32)) for...]
    pallas_call x2, Pallas kernels: 26.1 us -> 24 us  [one_row(): pl.pallas_call(row_kernel, name=name, out_shape=(jax.ShapeDtypeStruct((NN...]
  transfers between devices with their start and end apart: 2 -> 2, of which waited for: 1 -> 1; matrix products, arithmetic and copies ran while one was open for 1% -> 0% of each run, Pallas kernels for 8% -> 7%
where the time goes in v4:
time: 159 us; the launch traced here: 158 us
  Pallas kernels  131 us (82%)
  waiting for transfers between devices  12.2 us (8%)
  starting transfers between devices  6.85 us (4%)
  local copies, waits for them, and re-layouts  4.01 us (3%)
  other arithmetic  2.22 us (1%)
    pallas_call x1, Pallas kernels, gather(): pl.pallas_call(gather_kernel, name='gather', out_shape=jax.ShapeDtypeStru...  107 us
    pallas_call x2, Pallas kernels, one_row(): pl.pallas_call(row_kernel, name=name, out_shape=(jax.ShapeDtypeStruct((NN...  24 us
    ppermute x2, waiting for transfers between devices, on_device(): back.append(lax.ppermute(out, ('grp', 'dom'), pairs))  12.2 us
    ppermute x2, starting transfers between devices, on_device(): back.append(lax.ppermute(out, ('grp', 'dom'), pairs))  6.85 us
  transfers between devices with their start and end apart: 2, of which 1 were waited for; matrix products, arithmetic and copies ran while one was open for 0% of the time, Pallas kernels for 7%

profile of v4, /device:TPU:1, one launch (start us, length us, event | category | flops | bytes accessed | tf_op | source)
XLA Modules:
  0.0 158.5 jit_solution(16205379284138525636)
XLA Ops:
  0.8 0.8 constant_dynamic-slice_fusion
  1.6 0.1 copy.24
  1.7 0.1 eq.100
  1.8 0.1 broadcast_in_dim.134
  1.8 0.1 broadcast_in_dim.135
  2.0 0.9 convolution_convert_fusion
  2.9 0.1 copy.23
  2.9 0.7 select_reduce_fusion.2
  3.6 0.1 convert_reduce_fusion.1
  3.7 0.1 fusion.11
  3.9 0.1 copy.19
  4.0 0.1 select_reduce_fusion.3
  4.1 0.1 convert_reduce_fusion
  4.2 0.1 reshape.330
  4.3 0.1 select_reduce_fusion.1
  4.4 0.1 select_n.213
  4.5 0.2 fusion.4
  4.7 0.1 select_reduce_fusion
  4.9 0.1 concatenate.3
  5.0 107.3 %gather.1.all_ref = bf16[532,2,128,128]{3,2,1,0:T(8,128)(2,1)} custom-call(bf16[2,16,128,128]{3,2,1,0:T(8,128)(2,1)} %p_ref.1, bf16[2,16,128,128]{3,2,1,0:T(8,128)(2,1)} %h_ref.1), custom_call_target="tpu_custom_call" | custom-call | tf_op jit(solution)/shard_map/gather/pallas_call | solution.py:315
  112.3 12.5 %row0.1 = (f32[16,128,128]{2,1,0:T(8,128)S(1)}, f32[16,128,128]{2,1,0:T(8,128)S(1)}, bf16[2,16,128,128]{3,2,1,0:T(8,128)(2,1)S(1)}) custom-call(s32[643]{0:T(1024)S(1)} %get-tuple-element.15.table, bf16[532,2,128,128]{3,2,1,0:T(8,128)(2,1)} %gather.1.all_ref), custom_call_target="tpu_custom_call" | custom-call | flops 2617245696 | bytes 14680064 | tf_op jit(solution)/shard_map/row0/pallas_call | solution.py:408
  124.8 1.9 %collective-permute-start = (bf16[2,16,128,128]{3,2,1,0:T(8,128)(2,1)S(1)}, bf16[2,16,128,128]{3,2,1,0:T(8,128)(2,1)S(1)}, u32[]{:S(2)}, u32[]{:S(2)}) collective-permute-start(bf16[2,16,128,128]{3,2,1,0:T(8,128)(2,1)S(1)} %get-tuple-element.9), channel_id=1, source_target_pairs={{2,17},{3,16},{6,21},{7,20},{10,25},{11,24},{14,29},{15,28},{16,3}... | collective-permute-start | bytes 3145736 | tf_op jit(solution)/shard_map/ppermute | solution.py:498
  126.8 11.5 %row1.1 = (f32[16,128,128]{2,1,0:T(8,128)S(1)}, f32[16,128,128]{2,1,0:T(8,128)S(1)}, bf16[2,16,128,128]{3,2,1,0:T(8,128)(2,1)S(1)}) custom-call(s32[643]{0:T(1024)S(1)} %get-tuple-element.14.table, bf16[532,2,128,128]{3,2,1,0:T(8,128)(2,1)} %gather.1.all_ref), custom_call_target="tpu_custom_call" | custom-call | flops 2617245696 | bytes 14680064 | tf_op jit(solution)/shard_map/row1/pallas_call | solution.py:408
  138.3 4.9 %collective-permute-start.1 = (bf16[2,16,128,128]{3,2,1,0:T(8,128)(2,1)S(1)}, bf16[2,16,128,128]{3,2,1,0:T(8,128)(2,1)S(1)}, u32[]{:S(2)}, u32[]{:S(2)}) collective-permute-start(bf16[2,16,128,128]{3,2,1,0:T(8,128)(2,1)S(1)} %get-tuple-element.11), channel_id=1, source_target_pairs={{2,17},{3,16},{6,21},{7,20},{10,25},{11,24},{14,29},{15,28},{16,3}... | collective-permute-start | bytes 3145736 | tf_op jit(solution)/shard_map/ppermute | solution.py:498
  143.2 0.0 collective-permute-done
  143.2 0.3 convert_select_fusion.1
  143.5 12.2 %collective-permute-done.1 = bf16[2,16,128,128]{3,2,1,0:T(8,128)(2,1)S(1)} collective-permute-done((bf16[2,16,128,128]{3,2,1,0:T(8,128)(2,1)S(1)}, bf16[2,16,128,128]{3,2,1,0:T(8,128)(2,1)S(1)}, u32[]{:S(2)}, u32[]{:S(2)}) %collective-permute-start.1) | collective-permute-done | bytes 1048608 | tf_op jit(solution)/shard_map/ppermute | solution.py:498
  155.7 0.2 broadcast_in_dim.144
  155.9 0.2 broadcast_in_dim.142
  156.2 0.3 fusion.1
  156.5 0.0 copy-start
  156.5 0.0 copy-start.1
  156.5 1.3 copy-done
  157.8 0.7 copy-done.1
  (16 shorter events, 0.1 us)
Async XLA Ops:
  124.8 18.4 %collective-permute-start = (bf16[2,16,128,128]{3,2,1,0:T(8,128)(2,1)S(1)}, bf16[2,16,128,128]{3,2,1,0:T(8,128)(2,1)S(1)}, u32[]{:S(2)}, u32[]{:S(2)}) collective-permute-start(bf16[2,16,128,128]{3,2,1,0:T(8,128)(2,1)S(1)} %get-tuple-element.9), channel_id=1, source_target_pairs={{2,17},{3,16},{6,21},{7,20},{10,25},{11,24},{14,29},{15,28},{16,3}... | collective-permute-start | bytes 3145736 | tf_op jit(solution)/shard_map/ppermute | solution.py:498
  138.3 17.4 %collective-permute-start.1 = (bf16[2,16,128,128]{3,2,1,0:T(8,128)(2,1)S(1)}, bf16[2,16,128,128]{3,2,1,0:T(8,128)(2,1)S(1)}, u32[]{:S(2)}, u32[]{:S(2)}) collective-permute-start(bf16[2,16,128,128]{3,2,1,0:T(8,128)(2,1)S(1)} %get-tuple-element.11), channel_id=1, source_target_pairs={{2,17},{3,16},{6,21},{7,20},{10,25},{11,24},{14,29},{15,28},{16,3}... | collective-permute-start | bytes 3145736 | tf_op jit(solution)/shard_map/ppermute | solution.py:498
  156.5 1.3 copy-start
  156.5 2.0 %copy-start.1 = (f32[2,16,128,128]{3,2,1,0:T(8,128)}, f32[2,16,128,128]{3,2,1,0:T(8,128)S(1)}, u32[]{:S(2)}) copy-start(f32[2,16,128,128]{3,2,1,0:T(8,128)S(1)} %get-tuple-element.25) | copy-start | bytes 6291460

commit v5 on v4

--- a/solution.py
+++ b/solution.py
@@ -429,6 +429,48 @@
             flops=2 * 2 * 3 * 104 * BLK**3, bytes_accessed=14 << 20, transcendentals=0
         ),
     )(table, everything)
+
+
+def place_kernel(own, mine_x, mine_g, back, x_in, g_in, x_ref, g_ref, full, sem):
+    def store(src, k, q):
+        some = pl.ds(4 * q, 4)
+        return pltpu.make_async_copy(src.at[some], (x_ref, g_ref)[k].at[1, some], sem.at[k, q])
+
+    parts = [(k, q) for k in range(2) for q in range(4)]
+
+    @pl.when(own[0] == 1)
+    def _():
+        copies = [store((mine_x, mine_g)[k], k, q) for k, q in parts]
+        for copy in copies:
+            copy.start()
+        for copy in copies:
+            copy.wait()
+
+    @pl.when(own[0] == 0)
+    def _():
+        copies = []
+        for k, q in parts:
+            full[k, 4 * q : 4 * q + 4] = back[k, 4 * q : 4 * q + 4].astype(jnp.float32)
+            copies.append(store(full.at[k], k, q))
+            copies[-1].start()
+        for copy in copies:
+            copy.wait()
+
+
+def place(own, mine_x, mine_g, back, x, g):
+    whole = jax.ShapeDtypeStruct((2, NNZ, BLK, BLK), jnp.float32)
+    anywhere, vmem = pl.BlockSpec(memory_space=pl.ANY), pl.BlockSpec(memory_space=pltpu.VMEM)
+    return pl.pallas_call(
+        place_kernel,
+        name="place",
+        out_shape=(whole, whole),
+        in_specs=[pl.BlockSpec(memory_space=pltpu.SMEM), vmem, vmem, vmem, anywhere, anywhere],
+        out_specs=(anywhere, anywhere),
+        input_output_aliases={4: 0, 5: 1},
+        scratch_shapes=[pltpu.VMEM((2, NNZ, BLK, BLK), jnp.float32), pltpu.SemaphoreType.DMA((2, 4))],
+        compiler_params=pltpu.CompilerParams(vmem_limit_bytes=16 << 20),
+        cost_estimate=pl.CostEstimate(flops=1 << 20, bytes_accessed=4 << 20, transcendentals=0),
+    )(own, mine_x, mine_g, back, x, g)
 
 
 def tables(pattern, work_g, work_d):
@@ -496,12 +538,11 @@
         px, gx, out = one_row(f"row{w}", lists[w], everything)
         mine.append((px, gx))
         back.append(lax.ppermute(out, ("grp", "dom"), pairs))
-    res = []
+    firsts = []
     for k in range(2):
-        rows = [jnp.where(own, mine[w][k], back[w][k].astype(jnp.float32))[None] for w in range(2)]
-        both = jnp.broadcast_to(rows[0], (2, NNZ, BLK, BLK))
-        res.append(lax.dynamic_update_slice(both, rows[1], (1, 0, 0, 0)))
-    return tuple(res)
+        first = jnp.where(own, mine[0][k], back[0][k].astype(jnp.float32))
+        firsts.append(jnp.broadcast_to(first, (2, NNZ, BLK, BLK)))
+    return place(own.astype(jnp.int32).reshape(1), *mine[1], back[1], *firsts)
 
 
 def solution(mesh):

time: 159 us -> 166 us (1.044)
  Pallas kernels: 131 us -> 135 us
  local copies, waits for them, and re-layouts: 4.01 us -> 5.67 us
    broadcast_in_dim x2, local copies, waits for them, and re-layouts: 0.47 us -> 3.13 us  [on_device(): firsts.append(jnp.broadcast_to(first, (2, NNZ, BLK, BLK)))]
    pallas_call x0 -> x1, Pallas kernels: none -> 2.62 us  [place(): pl.pallas_call(place_kernel, name='place', out_shape=(whole, whole), in_s...]
  transfers between devices with their start and end apart: 2 -> 2, of which waited for: 1 -> 1; matrix products, arithmetic and copies ran while one was open for 0% -> 1% of each run, Pallas kernels for 7% -> 8%
where the time goes in v5:
time: 166 us; the launch traced here: 165 us
  Pallas kernels  135 us (81%)
  waiting for transfers between devices  11.3 us (7%)
  starting transfers between devices  7.79 us (5%)
  local copies, waits for them, and re-layouts  5.67 us (3%)
  other arithmetic  3.15 us (2%)
    pallas_call x1, Pallas kernels, gather(): pl.pallas_call(gather_kernel, name='gather', out_shape=jax.ShapeDtypeStru...  107 us
    pallas_call x2, Pallas kernels, one_row(): pl.pallas_call(row_kernel, name=name, out_shape=(jax.ShapeDtypeStruct((NN...  25.3 us
    ppermute x2, waiting for transfers between devices, on_device(): back.append(lax.ppermute(out, ('grp', 'dom'), pairs))  11.3 us
    ppermute x2, starting transfers between devices, on_device(): back.append(lax.ppermute(out, ('grp', 'dom'), pairs))  7.79 us
  transfers between devices with their start and end apart: 2, of which 1 were waited for; matrix products, arithmetic and copies ran while one was open for 1% of the time, Pallas kernels for 8%

profile of v5, /device:TPU:1, one launch (start us, length us, event | category | flops | bytes accessed | tf_op | source)
XLA Modules:
  0.0 165.0 jit_solution(16803612940670433922)
XLA Ops:
  0.8 0.8 constant_dynamic-slice_fusion
  1.5 0.1 copy.26
  1.6 0.1 eq.100
  1.8 0.9 convolution_convert_fusion
  2.7 0.1 copy.25
  2.8 0.7 select_reduce_fusion.2
  3.5 0.1 convert_reduce_fusion.1
  3.6 0.1 fusion.7
  3.7 0.1 select_reduce_fusion.3
  3.9 0.1 select_reduce_fusion.1
  4.0 0.1 select_n.204
  4.1 0.2 fusion
  4.3 0.1 reshape.331
  4.4 0.1 broadcast_in_dim.122
  4.4 0.1 broadcast_in_dim.123
  4.5 0.2 select_reduce_fusion
  4.7 0.1 convert_reduce_fusion
  4.8 0.1 copy.21
  4.9 0.1 concatenate.3
  5.0 107.3 %gather.1.all_ref = bf16[532,2,128,128]{3,2,1,0:T(8,128)(2,1)} custom-call(bf16[2,16,128,128]{3,2,1,0:T(8,128)(2,1)} %p_ref.1, bf16[2,16,128,128]{3,2,1,0:T(8,128)(2,1)} %h_ref.1), custom_call_target="tpu_custom_call" | custom-call | tf_op jit(solution)/shard_map/gather/pallas_call | solution.py:315
  112.3 12.7 %row0.1 = (f32[16,128,128]{2,1,0:T(8,128)S(1)}, f32[16,128,128]{2,1,0:T(8,128)S(1)}, bf16[2,16,128,128]{3,2,1,0:T(8,128)(2,1)}) custom-call(s32[643]{0:T(1024)S(1)} %get-tuple-element.14.table, bf16[532,2,128,128]{3,2,1,0:T(8,128)(2,1)} %gather.1.all_ref), custom_call_target="tpu_custom_call" | custom-call | flops 2617245696 | bytes 14680064 | tf_op jit(solution)/shard_map/row0/pallas_call | solution.py:408
  125.1 1.9 %collective-permute-start.1 = (bf16[2,16,128,128]{3,2,1,0:T(8,128)(2,1)}, bf16[2,16,128,128]{3,2,1,0:T(8,128)(2,1)}, u32[]{:S(2)}, u32[]{:S(2)}) collective-permute-start(bf16[2,16,128,128]{3,2,1,0:T(8,128)(2,1)} %get-tuple-element.12), channel_id=1, source_target_pairs={{2,17},{3,16},{6,21},{7,20},{10,25},{11,24},{14,29},{15,28},{16,3}... | collective-permute-start | bytes 3145736 | tf_op jit(solution)/shard_map/ppermute | solution.py:540
  127.0 12.6 %row1.1 = (f32[16,128,128]{2,1,0:T(8,128)S(1)}, f32[16,128,128]{2,1,0:T(8,128)S(1)}, bf16[2,16,128,128]{3,2,1,0:T(8,128)(2,1)}) custom-call(s32[643]{0:T(1024)S(1)} %get-tuple-element.15.table, bf16[532,2,128,128]{3,2,1,0:T(8,128)(2,1)} %gather.1.all_ref), custom_call_target="tpu_custom_call" | custom-call | flops 2617245696 | bytes 14680064 | tf_op jit(solution)/shard_map/row1/pallas_call | solution.py:408
  139.6 0.0 copy-start
  139.6 1.0 copy-done
  140.6 5.9 %collective-permute-start = (bf16[2,16,128,128]{3,2,1,0:T(8,128)(2,1)}, bf16[2,16,128,128]{3,2,1,0:T(8,128)(2,1)}, u32[]{:S(2)}, u32[]{:S(2)}) collective-permute-start(bf16[2,16,128,128]{3,2,1,0:T(8,128)(2,1)} %get-tuple-element.10), channel_id=1, source_target_pairs={{2,17},{3,16},{6,21},{7,20},{10,25},{11,24},{14,29},{15,28},{16,3}... | collective-permute-start | bytes 3145736 | tf_op jit(solution)/shard_map/ppermute | solution.py:540
  146.5 0.0 collective-permute-done.1
  146.5 1.5 convert_select_fusion
  147.9 11.3 %collective-permute-done.back = bf16[2,16,128,128]{3,2,1,0:T(8,128)(2,1)} collective-permute-done((bf16[2,16,128,128]{3,2,1,0:T(8,128)(2,1)}, bf16[2,16,128,128]{3,2,1,0:T(8,128)(2,1)}, u32[]{:S(2)}, u32[]{:S(2)}) %collective-permute-start) | collective-permute-done | bytes 1048608 | tf_op jit(solution)/shard_map/ppermute | solution.py:540
  159.2 1.6 broadcast_in_dim.130.x_in
  160.8 0.0 copy-start.1
  160.8 1.6 broadcast_in_dim.131.g_in
  162.4 0.0 copy-done.1
  162.4 2.6 %place.1 = (f32[2,16,128,128]{3,2,1,0:T(8,128)}, f32[2,16,128,128]{3,2,1,0:T(8,128)}) custom-call(s32[1]{0:T(128)} %bitcast.own, f32[16,128,128]{2,1,0:T(8,128)S(1)} %get-tuple-element.8.mine_x, f32[16,128,128]{2,1,0:T(8,128)S(1)} %copy-done.1, bf16[2,16,128,128]{3,2,1,0:T(8,128)(2,1)} %collective-permute-done.back, ...), custom_call_target="tpu_custom_call", output_to_operand_aliasing={{0}: (4, {}), {1}: (5, {})} | custom-call | flops 1048576 | bytes 4194304 | tf_op jit(solution)/shard_map/place/pallas_call | solution.py:463
  (16 shorter events, 0.1 us)
Async XLA Ops:
  125.1 21.4 %collective-permute-start.1 = (bf16[2,16,128,128]{3,2,1,0:T(8,128)(2,1)}, bf16[2,16,128,128]{3,2,1,0:T(8,128)(2,1)}, u32[]{:S(2)}, u32[]{:S(2)}) collective-permute-start(bf16[2,16,128,128]{3,2,1,0:T(8,128)(2,1)} %get-tuple-element.12), channel_id=1, source_target_pairs={{2,17},{3,16},{6,21},{7,20},{10,25},{11,24},{14,29},{15,28},{16,3}... | collective-permute-start | bytes 3145736 | tf_op jit(solution)/shard_map/ppermute | solution.py:540
  139.6 1.0 copy-start
  140.6 18.7 %collective-permute-start = (bf16[2,16,128,128]{3,2,1,0:T(8,128)(2,1)}, bf16[2,16,128,128]{3,2,1,0:T(8,128)(2,1)}, u32[]{:S(2)}, u32[]{:S(2)}) collective-permute-start(bf16[2,16,128,128]{3,2,1,0:T(8,128)(2,1)} %get-tuple-element.10), channel_id=1, source_target_pairs={{2,17},{3,16},{6,21},{7,20},{10,25},{11,24},{14,29},{15,28},{16,3}... | collective-permute-start | bytes 3145736 | tf_op jit(solution)/shard_map/ppermute | solution.py:540
  160.8 1.6 copy-start.1
